TPU v7x, 32 devices: a whole 2x2x4 slice. The times are simulated.
32 devices in a mesh: dp: 8 (over y, x, core), outer: 4 (over z).
Axes of the slice: x: 2, y: 2, z: 4, core: 2. Of those that a mesh axis runs over, the one named last changes fastest.
Arguments:
- images: bfloat16 [64, 144, 2048], P(('dp', 'outer')), may hold values from -27 to 27
- counts: int32 [32], replicated, may hold values from 1 to 2, as said below
- orientation: int32 [64], P(('dp', 'outer')), may hold values 0 or 1
- cotangent: bfloat16 [64, 144, 2048], P(('dp', 'outer')), may hold values from -6 to 6
- reducer: bfloat16 [2048, 512], replicated, may hold values from -0.125 to 0.125
- offseter: bfloat16 [4608, 18], replicated, may hold values from -0.125 to 0.125
- deformer: bfloat16 [4608, 512], replicated, may hold values from -0.09375 to 0.09375
- expander: bfloat16 [2048, 512], replicated, may hold values from -0.25 to 0.25
- narrower: bfloat16 [2048, 512], replicated, may hold values from -0.125 to 0.125
- convolver: bfloat16 [4608, 512], replicated, may hold values from -0.09375 to 0.09375
- widener: bfloat16 [2048, 512], replicated, may hold values from -0.25 to 0.25
- inner_gains: float32 [4, 512], replicated, may hold values from 0.5 to 1.5
- inner_biases: float32 [4, 512], replicated, may hold values from -2 to 2
- broad_gains: float32 [2, 2048], replicated, may hold values from 0.5 to 1.5
- broad_biases: float32 [2, 2048], replicated, may hold values from -2 to 2
Outputs:
- block_out: bfloat16 [64, 144, 2048], P(('dp', 'outer'))
- images_grad: bfloat16 [64, 144, 2048], P(('dp', 'outer'))
- reducer_grad: float32 [2048, 512], P('dp')
- offseter_grad: float32 [4608, 18], P('dp')
- deformer_grad: float32 [4608, 512], P('dp')
- expander_grad: float32 [2048, 512], P('dp')
- narrower_grad: float32 [2048, 512], P('dp')
- convolver_grad: float32 [4608, 512], P('dp')
- widener_grad: float32 [2048, 512], P('dp')
- inner_gains_grad: float32 [4, 512], P(None, 'dp')
- inner_biases_grad: float32 [4, 512], P(None, 'dp')
- broad_gains_grad: float32 [2, 2048], P(None, 'dp')
- broad_biases_grad: float32 [2, 2048], P(None, 'dp')
Inputs may be any that keep to these rules, and one draw needn't show every extreme that they name: `counts`: some device holds 2 live images and some holds 1; a device's live images fill its first slots. `orientation`: 0 marks a map of 4 rows and 36 columns, 1 one of 36 rows and 4 columns.
All inputs are finite; a program needn't handle non-finite values. No bound on the sum of `orientation` on one device may be relied on, other than what follows from the above.
Results may differ from a plain program's by a relative error of at most 0.018.
Values sent between devices are 32-bit elements; how exact they have to be, the bound alone decides.
A program may use at most 256 MiB of HBM per device.

v0:
```python
import jax
import jax.numpy as jnp
from jax import lax
from jax.sharding import PartitionSpec as P

CHANNELS = 2048
INNER = 512
TAPS = 9
SLOTS = 2
SHORT = 4
LONG = 36
PIXELS = 144


EPS = 1e-05
ROWS_TOGETHER = (((0,), (0,)), ((), ()))
LAST_TOGETHER = (((1,), (1,)), ((), ()))


def positions(width):
    pixel = jnp.arange(PIXELS, dtype=jnp.int32)
    return (pixel // width, pixel % width)


def tap_steps():
    tap = jnp.arange(TAPS, dtype=jnp.int32)
    return (2 * (tap // 3 - 1), 2 * (tap % 3 - 1))


def neighbours(height, width, sign):
    row, col = positions(width)
    step_y, step_x = tap_steps()
    near_y = row[:, None] + sign * step_y[None, :]
    near_x = col[:, None] + sign * step_x[None, :]
    inside = (near_y >= 0) & (near_y < height) & (near_x >= 0) & (near_x < width)
    index = jnp.clip(near_y, 0, height - 1) * width + jnp.clip(near_x, 0, width - 1)
    return (index, inside)


def gather_taps(field, height, width):
    index, inside = neighbours(height, width, 1)
    taken = field[index] * inside[:, :, None].astype(field.dtype)
    return taken.reshape(PIXELS, TAPS * field.shape[1])


def spread_taps(columns, height, width):
    index, inside = neighbours(height, width, -1)
    blocks = columns.reshape(PIXELS, TAPS, columns.shape[1] // TAPS)
    taken = blocks[index, jnp.arange(TAPS, dtype=jnp.int32)[None, :]]
    return jnp.sum(taken * inside[:, :, None].astype(jnp.float32), axis=1)


def sample(field, offsets, height, width):
    row, col = positions(width)
    step_y, step_x = tap_steps()
    pairs = offsets.reshape(PIXELS, TAPS, 2)
    frac_y = jax.nn.sigmoid(pairs[:, :, 0])
    frac_x = jax.nn.sigmoid(pairs[:, :, 1])
    corner_y = row[:, None] + step_y[None, :]
    corner_x = col[:, None] + step_x[None, :]
    total = jnp.zeros((PIXELS, TAPS, field.shape[1]), jnp.float32)
    for shift_y in (0, 1):
        for shift_x in (0, 1):
            near_y = corner_y + shift_y
            near_x = corner_x + shift_x
            weight_y = frac_y if shift_y == 1 else 1.0 - frac_y
            weight_x = frac_x if shift_x == 1 else 1.0 - frac_x
            inside = (near_y >= 0) & (near_y < height) & (near_x >= 0) & (near_x < width)
            index = jnp.clip(near_y, 0, height - 1) * width + jnp.clip(near_x, 0, width - 1)
            weight = weight_y * weight_x * inside.astype(jnp.float32)
            total = total + weight[:, :, None] * field[index]
    return total.reshape(PIXELS, TAPS * field.shape[1])


def silu_slope(value):
    sigma = jax.nn.sigmoid(value)
    return sigma * (1.0 + value * (1.0 - sigma))


def norm_forward(value, gain, bias, live, total):
    summed = lax.psum(jnp.sum(live * value, axis=0), ("dp", "outer"))
    mean = summed / total
    centered = value - mean
    spread = lax.psum(jnp.sum(live * centered * centered, axis=0), ("dp", "outer")) / total
    scale = lax.rsqrt(spread + EPS)
    normal = (value - mean) * scale
    return (normal, scale, normal * gain + bias)


def norm_backward(grad, normal, scale, gain, live, total):
    summed, paired = lax.psum(
        (jnp.sum(grad, axis=0), jnp.sum(grad * normal, axis=0)), ("dp", "outer")
    )
    back = gain * scale * (grad - live * (summed + normal * paired) / total)
    return (back.astype(jnp.bfloat16), summed, paired)


def per_device(
    images,
    counts,
    orientation,
    cotangent,
    reducer,
    offseter,
    deformer,
    expander,
    narrower,
    convolver,
    widener,
    inner_gains,
    inner_biases,
    broad_gains,
    broad_biases,
):
    rows = SLOTS * PIXELS
    device = lax.axis_index(("dp", "outer"))
    mine = lax.dynamic_index_in_dim(counts, device, keepdims=False)
    live_slots = (jnp.arange(SLOTS, dtype=jnp.int32) < mine).astype(jnp.float32)
    live = jnp.repeat(live_slots, PIXELS)[:, None]
    total = (jnp.sum(counts) * PIXELS).astype(jnp.float32)
    heights = SHORT + orientation * (LONG - SHORT)
    widths = LONG - orientation * (LONG - SHORT)
    flat = images.reshape(rows, CHANNELS)
    first = jnp.dot(flat, reducer, preferred_element_type=jnp.float32)
    norm_a, scale_a, pre_a = norm_forward(first, inner_gains[0], inner_biases[0], live, total)
    inner = jax.nn.silu(pre_a).astype(jnp.bfloat16)
    column_parts, offset_parts, sampled_parts = ([], [], [])
    for slot in range(SLOTS):
        field = inner[slot * PIXELS : (slot + 1) * PIXELS]
        columns = gather_taps(field, heights[slot], widths[slot])
        offsets = jnp.dot(columns, offseter, preferred_element_type=jnp.float32)
        sampled = sample(field.astype(jnp.float32), offsets, heights[slot], widths[slot]).astype(
            jnp.bfloat16
        )
        column_parts.append(columns)
        offset_parts.append(offsets)
        sampled_parts.append(sampled)
    columns_one = jnp.concatenate(column_parts, axis=0)
    sampled_all = jnp.concatenate(sampled_parts, axis=0)
    middle = jnp.dot(sampled_all, deformer, preferred_element_type=jnp.float32)
    norm_b, scale_b, pre_b = norm_forward(middle, inner_gains[1], inner_biases[1], live, total)
    hidden = jax.nn.silu(pre_b).astype(jnp.bfloat16)
    widened = lax.dot_general(hidden, expander, LAST_TOGETHER, preferred_element_type=jnp.float32)
    norm_c, scale_c, pre_c = norm_forward(widened, broad_gains[0], broad_biases[0], live, total)
    joined = pre_c + flat.astype(jnp.float32)
    between = jax.nn.silu(joined).astype(jnp.bfloat16)
    second = jnp.dot(between, narrower, preferred_element_type=jnp.float32)
    norm_d, scale_d, pre_d = norm_forward(second, inner_gains[2], inner_biases[2], live, total)
    narrow = jax.nn.silu(pre_d).astype(jnp.bfloat16)
    columns_two = jnp.concatenate(
        [
            gather_taps(narrow[slot * PIXELS : (slot + 1) * PIXELS], heights[slot], widths[slot])
            for slot in range(SLOTS)
        ],
        axis=0,
    )
    spatial = jnp.dot(columns_two, convolver, preferred_element_type=jnp.float32)
    norm_e, scale_e, pre_e = norm_forward(spatial, inner_gains[3], inner_biases[3], live, total)
    mixed = jax.nn.silu(pre_e).astype(jnp.bfloat16)
    final = lax.dot_general(mixed, widener, LAST_TOGETHER, preferred_element_type=jnp.float32)
    norm_f, scale_f, pre_f = norm_forward(final, broad_gains[1], broad_biases[1], live, total)
    joined_two = pre_f + between.astype(jnp.float32)
    block_out = (
        (live * jax.nn.silu(joined_two)).astype(jnp.bfloat16).reshape(SLOTS, PIXELS, CHANNELS)
    )
    upstream = cotangent.reshape(rows, CHANNELS).astype(jnp.float32) * live * silu_slope(joined_two)
    back_f, bias_f, gain_f = norm_backward(upstream, norm_f, scale_f, broad_gains[1], live, total)
    widener_part = lax.dot_general(back_f, mixed, ROWS_TOGETHER, preferred_element_type=jnp.float32)
    grad_mixed = jnp.dot(back_f, widener, preferred_element_type=jnp.float32)
    back_e, bias_e, gain_e = norm_backward(
        grad_mixed * silu_slope(pre_e), norm_e, scale_e, inner_gains[3], live, total
    )
    convolver_part = lax.dot_general(
        columns_two, back_e, ROWS_TOGETHER, preferred_element_type=jnp.float32
    )
    grad_columns = lax.dot_general(
        back_e, convolver, LAST_TOGETHER, preferred_element_type=jnp.float32
    )
    grad_narrow = jnp.concatenate(
        [
            spread_taps(
                grad_columns[slot * PIXELS : (slot + 1) * PIXELS], heights[slot], widths[slot]
            )
            for slot in range(SLOTS)
        ],
        axis=0,
    )
    back_d, bias_d, gain_d = norm_backward(
        grad_narrow * silu_slope(pre_d), norm_d, scale_d, inner_gains[2], live, total
    )
    narrower_part = lax.dot_general(
        between, back_d, ROWS_TOGETHER, preferred_element_type=jnp.float32
    )
    grad_between = upstream + lax.dot_general(
        back_d, narrower, LAST_TOGETHER, preferred_element_type=jnp.float32
    )
    narrower_grad, convolver_grad, widener_grad = (
        lax.psum_scatter(narrower_part, "dp", scatter_dimension=0, tiled=True),
        lax.psum_scatter(convolver_part, "dp", scatter_dimension=0, tiled=True),
        lax.psum_scatter(widener_part, "dp", scatter_dimension=0, tiled=True),
    )
    narrower_grad, convolver_grad, widener_grad = lax.psum(
        (narrower_grad, convolver_grad, widener_grad), "outer"
    )
    upstream_one = grad_between * silu_slope(joined)
    back_c, bias_c, gain_c = norm_backward(
        upstream_one, norm_c, scale_c, broad_gains[0], live, total
    )
    expander_part = lax.dot_general(
        back_c, hidden, ROWS_TOGETHER, preferred_element_type=jnp.float32
    )
    grad_hidden = jnp.dot(back_c, expander, preferred_element_type=jnp.float32)
    back_b, bias_b, gain_b = norm_backward(
        grad_hidden * silu_slope(pre_b), norm_b, scale_b, inner_gains[1], live, total
    )
    deformer_part = lax.dot_general(
        sampled_all, back_b, ROWS_TOGETHER, preferred_element_type=jnp.float32
    )
    grad_sampled = lax.dot_general(
        back_b, deformer, LAST_TOGETHER, preferred_element_type=jnp.float32
    ).astype(jnp.bfloat16)
    grad_inner_parts, grad_offset_parts = ([], [])
    for slot in range(SLOTS):
        field = inner[slot * PIXELS : (slot + 1) * PIXELS].astype(jnp.float32)
        offsets = offset_parts[slot]
        height = heights[slot]
        width = widths[slot]
        outcome, pullback = jax.vjp(
            lambda values, shifts: sample(values, shifts, height, width), field, offsets
        )
        grad_field, grad_shift = pullback(
            grad_sampled[slot * PIXELS : (slot + 1) * PIXELS].astype(jnp.float32)
        )
        grad_shift = grad_shift.astype(jnp.bfloat16)
        shift_columns = lax.dot_general(
            grad_shift, offseter, LAST_TOGETHER, preferred_element_type=jnp.float32
        )
        grad_inner_parts.append(grad_field + spread_taps(shift_columns, height, width))
        grad_offset_parts.append(grad_shift)
    grad_offsets = jnp.concatenate(grad_offset_parts, axis=0)
    offseter_part = lax.dot_general(
        columns_one, grad_offsets, ROWS_TOGETHER, preferred_element_type=jnp.float32
    )
    grad_inner = jnp.concatenate(grad_inner_parts, axis=0)
    back_a, bias_a, gain_a = norm_backward(
        grad_inner * silu_slope(pre_a), norm_a, scale_a, inner_gains[0], live, total
    )
    reducer_part = lax.dot_general(flat, back_a, ROWS_TOGETHER, preferred_element_type=jnp.float32)
    images_grad = (
        (
            upstream_one
            + lax.dot_general(back_a, reducer, LAST_TOGETHER, preferred_element_type=jnp.float32)
        )
        .astype(jnp.bfloat16)
        .reshape(SLOTS, PIXELS, CHANNELS)
    )
    reducer_grad, offseter_grad, deformer_grad, expander_grad = (
        lax.psum_scatter(reducer_part, "dp", scatter_dimension=0, tiled=True),
        lax.psum_scatter(offseter_part, "dp", scatter_dimension=0, tiled=True),
        lax.psum_scatter(deformer_part, "dp", scatter_dimension=0, tiled=True),
        lax.psum_scatter(expander_part, "dp", scatter_dimension=0, tiled=True),
    )
    reducer_grad, offseter_grad, deformer_grad, expander_grad = lax.psum(
        (reducer_grad, offseter_grad, deformer_grad, expander_grad), "outer"
    )
    inner_share = INNER // lax.axis_size("dp")
    broad_share = CHANNELS // lax.axis_size("dp")
    place = lax.axis_index("dp")
    inner_gains_grad = lax.dynamic_slice_in_dim(
        jnp.stack([gain_a, gain_b, gain_d, gain_e]), place * inner_share, inner_share, 1
    )
    inner_biases_grad = lax.dynamic_slice_in_dim(
        jnp.stack([bias_a, bias_b, bias_d, bias_e]), place * inner_share, inner_share, 1
    )
    broad_gains_grad = lax.dynamic_slice_in_dim(
        jnp.stack([gain_c, gain_f]), place * broad_share, broad_share, 1
    )
    broad_biases_grad = lax.dynamic_slice_in_dim(
        jnp.stack([bias_c, bias_f]), place * broad_share, broad_share, 1
    )
    return (
        block_out,
        images_grad,
        reducer_grad,
        offseter_grad,
        deformer_grad,
        expander_grad,
        narrower_grad,
        convolver_grad,
        widener_grad,
        inner_gains_grad,
        inner_biases_grad,
        broad_gains_grad,
        broad_biases_grad,
    )


def solution(mesh):
    in_specs = (
        P(("dp", "outer"), None, None),
        P(),
        P(("dp", "outer")),
        P(("dp", "outer"), None, None),
        P(),
        P(),
        P(),
        P(),
        P(),
        P(),
        P(),
        P(),
        P(),
        P(),
        P(),
    )
    out_specs = (
        P(("dp", "outer"), None, None),
        P(("dp", "outer"), None, None),
        P("dp", None),
        P("dp", None),
        P("dp", None),
        P("dp", None),
        P("dp", None),
        P("dp", None),
        P("dp", None),
        P(None, "dp"),
        P(None, "dp"),
        P(None, "dp"),
        P(None, "dp"),
    )
    return jax.shard_map(
        per_device, mesh=mesh, in_specs=in_specs, out_specs=out_specs, check_vma=False
    )
```

profile of v0, /device:TPU:0, one launch (start us, length us, event | category | flops | bytes accessed | tf_op | source)
XLA Modules:
  0.0 1778.6 jit_solution(14767407104846815152)
XLA Ops:
  40.8 42.0 %psum.217 = f32[512]{0:T(512)S(1)} all-reduce(f32[512]{0:T(512)S(1)} %get-tuple-element.188), channel_id=1, replica_groups=mesh['dp'=8,'outer'=4] {'dp','outer'}, use_global_device_ids=true, to_apply=%region_1.2 | all-reduce | flops 512 | bytes 4096 | tf_op jit(solution)/shard_map/psum | solution.py:81
  83.0 40.6 %psum.218 = f32[512]{0:T(512)S(1)} all-reduce(f32[512]{0:T(512)S(1)} %fusion.9), channel_id=1, replica_groups=mesh['dp'=8,'outer'=4] {'dp','outer'}, use_global_device_ids=true, to_apply=%region_4.5 | all-reduce | flops 512 | bytes 4096 | tf_op jit(solution)/shard_map/psum | solution.py:84
  262.2 40.0 %psum.219 = f32[512]{0:T(512)S(1)} all-reduce(f32[512]{0:T(512)S(1)} %get-tuple-element.190), channel_id=1, replica_groups=mesh['dp'=8,'outer'=4] {'dp','outer'}, use_global_device_ids=true, to_apply=%region_6.7 | all-reduce | flops 512 | bytes 4096 | tf_op jit(solution)/shard_map/psum | solution.py:81
  302.4 40.1 %psum.220 = f32[512]{0:T(512)S(1)} all-reduce(f32[512]{0:T(512)S(1)} %fusion.10), channel_id=1, replica_groups=mesh['dp'=8,'outer'=4] {'dp','outer'}, use_global_device_ids=true, to_apply=%region_8.9 | all-reduce | flops 512 | bytes 4096 | tf_op jit(solution)/shard_map/psum | solution.py:84
  346.9 40.1 %psum.221 = f32[2048]{0:T(1024)S(1)} all-reduce(f32[2048]{0:T(1024)S(1)} %get-tuple-element.192), channel_id=1, replica_groups=mesh['dp'=8,'outer'=4] {'dp','outer'}, use_global_device_ids=true, to_apply=%region_10.11 | all-reduce | flops 2048 | bytes 16384 | tf_op jit(solution)/shard_map/psum | solution.py:81
  389.1 40.1 %psum.222 = f32[2048]{0:T(1024)S(1)} all-reduce(f32[2048]{0:T(1024)S(1)} %fusion.6), channel_id=1, replica_groups=mesh['dp'=8,'outer'=4] {'dp','outer'}, use_global_device_ids=true, to_apply=%region_12.13 | all-reduce | flops 2048 | bytes 16384 | tf_op jit(solution)/shard_map/psum | solution.py:84
  433.7 40.1 %psum.223 = f32[512]{0:T(512)S(1)} all-reduce(f32[512]{0:T(512)S(1)} %get-tuple-element.194), channel_id=1, replica_groups=mesh['dp'=8,'outer'=4] {'dp','outer'}, use_global_device_ids=true, to_apply=%region_14.15 | all-reduce | flops 512 | bytes 4096 | tf_op jit(solution)/shard_map/psum | solution.py:81
  473.9 40.4 %psum.224 = f32[512]{0:T(512)S(1)} all-reduce(f32[512]{0:T(512)S(1)} %fusion.11), channel_id=1, replica_groups=mesh['dp'=8,'outer'=4] {'dp','outer'}, use_global_device_ids=true, to_apply=%region_16.17 | all-reduce | flops 512 | bytes 4096 | tf_op jit(solution)/shard_map/psum | solution.py:84
  545.4 40.1 %psum.225 = f32[512]{0:T(512)S(1)} all-reduce(f32[512]{0:T(512)S(1)} %get-tuple-element.196), channel_id=1, replica_groups=mesh['dp'=8,'outer'=4] {'dp','outer'}, use_global_device_ids=true, to_apply=%region_18.19 | all-reduce | flops 512 | bytes 4096 | tf_op jit(solution)/shard_map/psum | solution.py:81
  585.7 40.0 %psum.226 = f32[512]{0:T(512)S(1)} all-reduce(f32[512]{0:T(512)S(1)} %fusion.12), channel_id=1, replica_groups=mesh['dp'=8,'outer'=4] {'dp','outer'}, use_global_device_ids=true, to_apply=%region_20.21 | all-reduce | flops 512 | bytes 4096 | tf_op jit(solution)/shard_map/psum | solution.py:84
  630.2 40.1 %psum.227 = f32[2048]{0:T(1024)S(1)} all-reduce(f32[2048]{0:T(1024)S(1)} %get-tuple-element.198), channel_id=1, replica_groups=mesh['dp'=8,'outer'=4] {'dp','outer'}, use_global_device_ids=true, to_apply=%region_22.23 | all-reduce | flops 2048 | bytes 16384 | tf_op jit(solution)/shard_map/psum | solution.py:81
  672.3 40.1 %psum.228 = f32[2048]{0:T(1024)S(1)} all-reduce(f32[2048]{0:T(1024)S(1)} %fusion.7), channel_id=1, replica_groups=mesh['dp'=8,'outer'=4] {'dp','outer'}, use_global_device_ids=true, to_apply=%region_24.25 | all-reduce | flops 2048 | bytes 16384 | tf_op jit(solution)/shard_map/psum | solution.py:84
  717.0 40.4 %all-reduce.9 = (f32[2048]{0:T(1024)S(1)}, f32[2048]{0:T(1024)S(1)}) all-reduce(f32[2048]{0:T(1024)S(1)} %get-tuple-element.76, f32[2048]{0:T(1024)S(1)} %get-tuple-element.75), channel_id=1, replica_groups=mesh['dp'=8,'outer'=4] {'dp','outer'}, use_global_device_ids=true, to_apply=%region_28.29 | all-reduce | flops 4096 | bytes 32768 | tf_op jit(solution)/shard_map/psum | solution.py:91
  771.9 40.0 %all-reduce.8 = (f32[512]{0:T(512)S(1)}, f32[512]{0:T(512)S(1)}) all-reduce(f32[512]{0:T(512)S(1)} %get-tuple-element.84, f32[512]{0:T(512)S(1)} %get-tuple-element.83), channel_id=1, replica_groups=mesh['dp'=8,'outer'=4] {'dp','outer'}, use_global_device_ids=true, to_apply=%region_32.33 | all-reduce | flops 1024 | bytes 8192 | tf_op jit(solution)/shard_map/psum | solution.py:91
  822.1 29.1 %gather_fusion.13 = f32[1296,512]{1,0:T(8,128)} fusion(f32[144,9,512]{2,0,1:T(8,128)} %bitcast.192, s32[1296]{0:T(1024)S(1)} %reshape.3017), kind=kCustom, calls=%fused_computation.13 | custom fusion | bytes 5318784 | tf_op jit(solution)/shard_map/gather | solution.py:49
  855.6 29.1 %gather_fusion.12 = f32[1296,512]{1,0:T(8,128)} fusion(f32[144,9,512]{2,0,1:T(8,128)} %bitcast.191, s32[1296]{0:T(1024)S(1)} %reshape.3011), kind=kCustom, calls=%fused_computation.12 | custom fusion | bytes 5318784 | tf_op jit(solution)/shard_map/gather | solution.py:49
  895.1 40.5 %all-reduce.7 = (f32[512]{0:T(512)S(1)}, f32[512]{0:T(512)S(1)}) all-reduce(f32[512]{0:T(512)S(1)} %get-tuple-element.82, f32[512]{0:T(512)S(1)} %get-tuple-element.81), channel_id=1, replica_groups=mesh['dp'=8,'outer'=4] {'dp','outer'}, use_global_device_ids=true, to_apply=%region_38.39 | all-reduce | flops 1024 | bytes 8192 | tf_op jit(solution)/shard_map/psum | solution.py:91
  943.8 40.0 %all-reduce.6 = (f32[2048]{0:T(1024)S(1)}, f32[2048]{0:T(1024)S(1)}) all-reduce(f32[2048]{0:T(1024)S(1)} %get-tuple-element.74, f32[2048]{0:T(1024)S(1)} %get-tuple-element.73), channel_id=1, replica_groups=mesh['dp'=8,'outer'=4] {'dp','outer'}, use_global_device_ids=true, to_apply=%region_42.43 | all-reduce | flops 4096 | bytes 32768 | tf_op jit(solution)/shard_map/psum | solution.py:91
  997.3 40.6 %all-reduce.5 = (f32[512]{0:T(512)S(1)}, f32[512]{0:T(512)S(1)}) all-reduce(f32[512]{0:T(512)S(1)} %get-tuple-element.80, f32[512]{0:T(512)S(1)} %get-tuple-element.79), channel_id=1, replica_groups=mesh['dp'=8,'outer'=4] {'dp','outer'}, use_global_device_ids=true, to_apply=%region_46.47 | all-reduce | flops 1024 | bytes 8192 | tf_op jit(solution)/shard_map/psum | solution.py:91
  1292.9 40.5 %all-reduce.4 = (f32[512]{0:T(512)S(1)}, f32[512]{0:T(512)S(1)}) all-reduce(f32[512]{0:T(512)S(1)} %get-tuple-element.78, f32[512]{0:T(512)S(1)} %get-tuple-element.77), channel_id=1, replica_groups=mesh['dp'=8,'outer'=4] {'dp','outer'}, use_global_device_ids=true, to_apply=%region_68.69 | all-reduce | flops 1024 | bytes 8192 | tf_op jit(solution)/shard_map/psum | solution.py:91
  1388.8 79.9 %reduce-scatter.12.cloned.1.call-done = f32[576,512]{1,0:T(8,128)} async-done(((f32[4608,512]{1,0:T(8,128)}), f32[576,512]{1,0:T(8,128)}) %reduce-scatter.12.cloned.1.call-update) | async-done | bytes 1179664 | tf_op jit(solution)/shard_map/reduce_scatter | solution.py:260
  1468.7 79.9 %reduce-scatter.18.cloned.1.call-done = f32[576,512]{1,0:T(8,128)} async-done(((f32[4608,512]{1,0:T(8,128)}), f32[576,512]{1,0:T(8,128)}) %reduce-scatter.18.cloned.1.call-update) | async-done | bytes 1179664 | tf_op jit(solution)/shard_map/reduce_scatter | solution.py:199
  1555.4 39.0 %reduce-scatter.22.cloned.1.call-done = f32[576,18]{1,0:T(8,128)} async-done(((f32[4608,18]{1,0:T(8,128)}), f32[576,18]{1,0:T(8,128)}) %reduce-scatter.22.cloned.1.call-update) | async-done | bytes 41488
  1617.2 146.4 %all-reduce.13.cloned.1.call-done = (f32[256,512]{0,1:T(8,128)}, f32[576,512]{1,0:T(8,128)}, f32[256,512]{1,0:T(8,128)}, f32[256,512]{1,0:T(8,128)}, f32[576,512]{1,0:T(8,128)}, /*index=5*/f32[256,512]{1,0:T(8,128)}) async-done(((f32[256,512]{0,1:T(8,128)}, f32[576,512]{1,0:T(8,128)}, f32[256,512]{1,0:T(8,128)}, f32[256,512]{1,0:T(8,128)}, f32[576,512]{1,0:T(8,128)}, /*index=5*/f32[256,512]{1,0:T(8,128)}), ...) | async-done | bytes 4456464 | tf_op jit(solution)/shard_map/psum | solution.py:263
  (514 shorter events, 626.3 us)
Async XLA Ops:
  7.2 425.5 %copy-start = (bf16[2048,512]{1,0:T(8,128)(2,1)S(1)}, bf16[2048,512]{1,0:T(8,128)(2,1)}, u32[]{:S(2)}) copy-start(bf16[2048,512]{1,0:T(8,128)(2,1)} %param.23) | copy-start | bytes 6291460
  7.2 1354.2 %reduce-scatter.20.cloned.1.call-start = ((), (), s32[]{:S(2)}) async-start(), calls=%async_computation.12 | async-start | bytes 4718592 | tf_op jit(solution)/shard_map/reduce_scatter | solution.py:200
  12.5 150.1 %copy-start.99 = (s32[9]{0:T(128)}, s32[9]{0:T(128)S(1)}, u32[]{:S(2)}) copy-start(s32[9]{0:T(128)S(1)} %get-tuple-element.207) | copy-start | bytes 112
  12.5 150.1 %copy-start.101 = (s32[9]{0:T(128)}, s32[9]{0:T(128)S(1)}, u32[]{:S(2)}) copy-start(s32[9]{0:T(128)S(1)} %get-tuple-element.208) | copy-start | bytes 112
  19.0 143.5 %copy-start.95 = (s32[144]{0:T(256)}, s32[144]{0:T(256)S(1)}, u32[]{:S(2)}) copy-start(s32[144]{0:T(256)S(1)} %and_select_fusion.3) | copy-start | bytes 1732
  19.9 142.7 %copy-start.97 = (s32[144]{0:T(256)}, s32[144]{0:T(256)S(1)}, u32[]{:S(2)}) copy-start(s32[144]{0:T(256)S(1)} %and_select_fusion.5) | copy-start | bytes 1732
  585.6 175.0 %copy-start.67 = (f32[512]{0:T(512)}, f32[512]{0:T(512)S(1)}, u32[]{:S(2)}) copy-start(f32[512]{0:T(512)S(1)} %broadcast_divide_fusion.2) | copy-start | bytes 6148
  765.0 596.4 %reduce-scatter.14.cloned.1.call-start = ((), (), s32[]{:S(2)}) async-start(), calls=%async_computation.9 | async-start | bytes 4718592 | tf_op jit(solution)/shard_map/reduce_scatter | solution.py:261
  990.4 371.0 %reduce-scatter.16.cloned.1.call-start = ((), (), s32[]{:S(2)}) async-start(), calls=%async_computation.10 | async-start | bytes 4718592 | tf_op jit(solution)/shard_map/reduce_scatter | solution.py:198
  994.7 394.2 %reduce-scatter.10.cloned.1.call-start = ((), (), s32[]{:S(2)}) async-start(), calls=%async_computation.7 | async-start | bytes 4718592 | tf_op jit(solution)/shard_map/reduce_scatter | solution.py:258
  1337.0 131.7 %reduce-scatter.12.cloned.1.call-start = ((), (), s32[]{:S(2)}) async-start(), calls=%async_computation.8 | async-start | bytes 10616832 | tf_op jit(solution)/shard_map/reduce_scatter | solution.py:260
  1344.9 203.7 %reduce-scatter.18.cloned.1.call-start = ((), (), s32[]{:S(2)}) async-start(), calls=%async_computation.11 | async-start | bytes 10616832 | tf_op jit(solution)/shard_map/reduce_scatter | solution.py:199
  1353.2 241.3 %reduce-scatter.22.cloned.1.call-start = ((), (), s32[]{:S(2)}) async-start(), calls=%async_computation.13 | async-start | bytes 2654208
  1361.2 187.4 %copy-start.72 = (f32[2048]{0:T(1024)S(1)}, f32[2048]{0:T(1024)}, u32[]{:S(2)}) copy-start(f32[2048]{0:T(1024)} %copy-done.71) | copy-start | bytes 24580
  1361.2 187.4 %copy-start.76 = (f32[2048]{0:T(1024)S(1)}, f32[2048]{0:T(1024)}, u32[]{:S(2)}) copy-start(f32[2048]{0:T(1024)} %copy-done.75) | copy-start | bytes 24580
  1361.2 188.1 %copy-start.70 = (f32[2048]{0:T(1024)S(1)}, f32[2048]{0:T(1024)}, u32[]{:S(2)}) copy-start(f32[2048]{0:T(1024)} %copy-done.69) | copy-start | bytes 24580
  1361.2 188.1 %copy-start.74 = (f32[2048]{0:T(1024)S(1)}, f32[2048]{0:T(1024)}, u32[]{:S(2)}) copy-start(f32[2048]{0:T(1024)} %copy-done.73) | copy-start | bytes 24580
  1361.2 188.7 %copy-start.121 = (f32[512]{0:T(512)S(1)}, f32[512]{0:T(512)}, u32[]{:S(2)}) copy-start(f32[512]{0:T(512)} %copy-done.120) | copy-start | bytes 6148
  1361.2 188.7 %copy-start.125 = (f32[512]{0:T(512)S(1)}, f32[512]{0:T(512)}, u32[]{:S(2)}) copy-start(f32[512]{0:T(512)} %copy-done.124) | copy-start | bytes 6148
  1361.2 188.7 %copy-start.129 = (f32[512]{0:T(512)S(1)}, f32[512]{0:T(512)}, u32[]{:S(2)}) copy-start(f32[512]{0:T(512)} %copy-done.128) | copy-start | bytes 6148
  1361.2 189.3 %copy-start.119 = (f32[512]{0:T(512)S(1)}, f32[512]{0:T(512)}, u32[]{:S(2)}) copy-start(f32[512]{0:T(512)} %copy-done.118) | copy-start | bytes 6148
  1361.3 189.3 %copy-start.123 = (f32[512]{0:T(512)S(1)}, f32[512]{0:T(512)}, u32[]{:S(2)}) copy-start(f32[512]{0:T(512)} %copy-done.122) | copy-start | bytes 6148
  1361.3 189.3 %copy-start.127 = (f32[512]{0:T(512)S(1)}, f32[512]{0:T(512)}, u32[]{:S(2)}) copy-start(f32[512]{0:T(512)} %copy-done.126) | copy-start | bytes 6148
  1361.3 402.3 %all-reduce.13.cloned.1.call-start = ((), (), s32[]{:S(2)}) async-start(), calls=%async_computation.14 | async-start | bytes 8912896 | tf_op jit(solution)/shard_map/psum | solution.py:263
  (117 other events, 3438.1 us)
Sparse Core Ops, SparseCore 0:
  765.1 51.8 reduce-scatter.19
  990.6 52.5 reduce-scatter.13
  1046.5 51.1 reduce-scatter.15
  1337.1 51.7 reduce-scatter.9
  1392.2 76.4 reduce-scatter.11
  1472.1 76.4 reduce-scatter.17
  1551.9 42.4 reduce-scatter.21
  1597.5 166.0 all-reduce.12
where the time goes:
time: 1790 us; the launch traced here: 1780 us
  blocking collectives  748 us (42%)
  waiting for transfers between devices  373 us (21%)
  local copies, waits for them, and re-layouts  350 us (20%)
  other arithmetic  202 us (11%)
  matrix products  83.4 us (5%)
  between operations  23.1 us (1%)
    psum x6, blocking collectives, norm_forward(): summed = lax.psum(jnp.sum(live * value, axis=0), ('dp', 'outer'))  242 us
    psum x6, blocking collectives, norm_backward(): lax.psum((jnp.sum(grad, axis=0), jnp.sum(grad * normal, axis=0)), ('dp',...  242 us
    psum x6, blocking collectives, norm_forward(): lax.psum(jnp.sum(live * centered * centered, axis=0), ('dp', 'outer'))  241 us
    psum x1, waiting for transfers between devices, per_device(): lax.psum((reducer_grad, offseter_grad, deformer_grad, expander_grad), 'ou...  146 us
    gather x8, local copies, waits for them, and re-layouts, spread_taps(): taken = blocks[index, jnp.arange(TAPS, dtype=jnp.int32)[None, :]]  134 us
    scatter-add x8, other arithmetic, sample(): total = total + weight[:, :, None] * field[index]  83.5 us
    reduce_scatter x1, waiting for transfers between devices, per_device(): lax.psum_scatter(convolver_part, 'dp', scatter_dimension=0, tiled=True)  79.9 us
    reduce_scatter x1, waiting for transfers between devices, per_device(): lax.psum_scatter(deformer_part, 'dp', scatter_dimension=0, tiled=True)  79.9 us
  transfers between devices with their start and end apart: 8, of which 5 were waited for; matrix products, arithmetic and copies ran while one was open for 22% of the time, Pallas kernels for 0%

commit v1 on v0

v1 whole, which is shorter than its diff:
```python
import functools

import jax
import jax.numpy as jnp
from jax import lax
from jax.experimental import pallas as pl
from jax.experimental.pallas import tpu as pltpu
from jax.sharding import PartitionSpec as P

CHANNELS = 2048
INNER = 512
TAPS = 9
SLOTS = 2
SHORT = 4
LONG = 36
PIXELS = 144
ROWS = SLOTS * PIXELS
OFFSETS = 2 * TAPS
EPS = 1e-05
BF = jnp.bfloat16
F32 = jnp.float32
MESH = pl.DeviceIdType.MESH
NN = (((1,), (0,)), ((), ()))
NT = (((1,), (1,)), ((), ()))
TN = (((0,), (0,)), ((), ()))
INPUTS = [
    "counts",
    "orient",
    "ig",
    "ib",
    "bg",
    "bb",
    "images_h",
    "cot_h",
    "red_h",
    "off_h",
    "def_h",
    "exp_h",
    "nar_h",
    "con_h",
    "wid_h",
]
OUTPUTS = [
    "out_h",
    "grad_h",
    "g_red",
    "g_off",
    "g_def",
    "g_exp",
    "g_nar",
    "g_con",
    "g_wid",
    "g_ig",
    "g_ib",
    "g_bg",
    "g_bb",
]


def mm(left, right, dims):
    return lax.dot_general(left, right, dims, preferred_element_type=F32)


def sigmoid(value):
    return 0.5 * jnp.tanh(0.5 * value) + 0.5


def fold(value):
    return jnp.sum(value.reshape(value.shape[0] // 8, 8, value.shape[1]), axis=0)


def total_row(value):
    return jnp.sum(value, axis=0, keepdims=True)


def scratch(dp, outer):
    vmem = pltpu.VMEM
    dma = pltpu.SemaphoreType.DMA
    return dict(
        images=vmem((ROWS, CHANNELS), BF),
        cot=vmem((ROWS, CHANNELS), BF),
        red=vmem((CHANNELS, INNER), BF),
        off=vmem((TAPS * INNER, OFFSETS), BF),
        dfm=vmem((TAPS * INNER, INNER), BF),
        exp=vmem((CHANNELS, INNER), BF),
        nar=vmem((CHANNELS, INNER), BF),
        con=vmem((TAPS * INNER, INNER), BF),
        wid=vmem((CHANNELS, INNER), BF),
        a1=vmem((ROWS, INNER), F32),
        a2=vmem((ROWS, INNER), F32),
        b1=vmem((ROWS, INNER), F32),
        b2=vmem((ROWS, INNER), F32),
        acc=vmem((ROWS, INNER), F32),
        a3=vmem((ROWS, CHANNELS), F32),
        b3=vmem((ROWS, CHANNELS), F32),
        up=vmem((ROWS, CHANNELS), F32),
        inner=vmem((ROWS, INNER), BF),
        hidden=vmem((ROWS, INNER), BF),
        narrow=vmem((ROWS, INNER), BF),
        mixed=vmem((ROWS, INNER), BF),
        dn=vmem((ROWS, INNER), BF),
        turned=vmem((ROWS, INNER), BF),
        between=vmem((ROWS, CHANNELS), BF),
        dwide=vmem((ROWS, CHANNELS), BF),
        obuf=vmem((ROWS, CHANNELS), BF),
        samp=vmem((TAPS, ROWS, INNER), BF),
        cols=vmem((TAPS, ROWS, INNER), BF),
        wmat=vmem((SLOTS, TAPS, PIXELS, PIXELS), BF),
        tmat=vmem((SLOTS, TAPS, PIXELS, PIXELS), BF),
        geo=vmem((SLOTS, 2, PIXELS, PIXELS), jnp.int32),
        frac=vmem((ROWS, OFFSETS), F32),
        doff=vmem((ROWS, OFFSETS), F32),
        ogt=vmem((OFFSETS, TAPS * INNER), F32),
        stage=vmem((2, 512, 512), F32),
        stn=vmem((4, 2, INNER), F32),
        stw=vmem((2, 2, CHANNELS), F32),
        rxn1=vmem((8, dp, 2, INNER), F32),
        rxn2=vmem((8, outer, 2, INNER), F32),
        rxw1=vmem((4, dp, 2, CHANNELS), F32),
        rxw2=vmem((4, outer, 2, CHANNELS), F32),
        load_sem=dma((9,)),
        stage_sem=dma((2,)),
        out_sem=dma((3,)),
        send1=dma((12,)),
        recv1=dma((12,)),
        send2=dma((12,)),
        recv2=dma((12,)),
    )


def kernel(dp, outer, names, *refs):
    r = dict(zip(names, refs))
    me = lax.axis_index("dp")
    mine = lax.axis_index("outer")
    counts, orient = r["counts"], r["orient"]

    loads = {}
    for place, (source, target) in enumerate(
        (
            ("images_h", "images"),
            ("red_h", "red"),
            ("off_h", "off"),
            ("def_h", "dfm"),
            ("exp_h", "exp"),
            ("nar_h", "nar"),
            ("con_h", "con"),
            ("wid_h", "wid"),
            ("cot_h", "cot"),
        )
    ):
        loads[target] = pltpu.make_async_copy(r[source], r[target], r["load_sem"].at[place])
        loads[target].start()

    barrier = pltpu.get_barrier_semaphore()
    for step in range(1, dp):
        pl.semaphore_signal(
            barrier, inc=1, device_id=(lax.rem(me + step, dp), mine), device_id_type=MESH
        )
    for step in range(1, outer):
        pl.semaphore_signal(
            barrier, inc=1, device_id=(me, lax.rem(mine + step, outer)), device_id_type=MESH
        )

    def images_of(first, second):
        return counts[first * outer + second].astype(F32)

    near = jnp.zeros((dp, 1), F32)
    line = lax.broadcasted_iota(jnp.int32, (dp, 1), 0)
    for place in range(dp):
        near = near + jnp.where(line == place, images_of(place, mine), 0.0)
    near = near * float(PIXELS)
    far = jnp.zeros((outer, 1), F32)
    line = lax.broadcasted_iota(jnp.int32, (outer, 1), 0)
    for place in range(outer):
        group = images_of(0, place)
        for other in range(1, dp):
            group = group + images_of(other, place)
        far = far + jnp.where(line == place, group, 0.0)
    far = far * float(PIXELS)
    near_total = total_row(near)
    total = total_row(far)
    held = images_of(me, mine)
    live1 = held - 1.0
    local = held * float(PIXELS)

    def sweep(body, init):
        def step(i, carry):
            lv = jnp.where(i < 3, 1.0, live1)
            for j in range(3):
                carry = body(pl.ds(pl.multiple_of(i * 48 + j * 16, 16), 16), lv, carry)
            return carry

        return lax.fori_loop(0, 6, step, init)

    def several(count, count_bytes_of, sem):
        view = count_bytes_of.at[pl.ds(0, count)]
        return pltpu.make_async_copy(view, view, sem)

    pending = []

    def exchange(number, rx1, rx2, forward):
        for step in range(1, dp):
            pltpu.make_async_remote_copy(
                src_ref=rx1.at[me],
                dst_ref=rx1.at[me],
                send_sem=r["send1"].at[number],
                recv_sem=r["recv1"].at[number],
                device_id=(lax.rem(me + step, dp), mine),
                device_id_type=MESH,
            ).start()
        pending.append((dp - 1, rx1, r["send1"].at[number]))
        several(dp - 1, rx1, r["recv1"].at[number]).wait()
        rx2[mine] = merge(rx1, near, near_total, forward)
        for step in range(1, outer):
            pltpu.make_async_remote_copy(
                src_ref=rx2.at[mine],
                dst_ref=rx2.at[mine],
                send_sem=r["send2"].at[number],
                recv_sem=r["recv2"].at[number],
                device_id=(me, lax.rem(mine + step, outer)),
                device_id_type=MESH,
            ).start()
        pending.append((outer - 1, rx2, r["send2"].at[number]))
        several(outer - 1, rx2, r["recv2"].at[number]).wait()
        return merge(rx2, far, total, forward)

    def merge(rx, sizes, size, forward):
        first = rx[:, 0, :]
        second = rx[:, 1, :]
        if forward:
            summed = total_row(first)
            apart = first / sizes - summed / size
            spread = total_row(second + sizes * apart * apart)
            return jnp.concatenate([summed, spread], axis=0)
        return jnp.concatenate([total_row(first), total_row(second)], axis=0)

    def norm_stats(ref, width, number, rx1, rx2, st):
        for start in range(0, width, 512):
            cs = pl.ds(start, 512)
            zero = jnp.zeros((8, 512), F32)
            summed = total_row(sweep(lambda rs, lv, c: c + lv * fold(ref[rs, cs]), zero))
            mean = summed / local

            def squares(rs, lv, carry):
                apart = ref[rs, cs] - mean
                return carry + lv * fold(apart * apart)

            spread = total_row(sweep(squares, zero))
            rx1[me, 0:1, cs] = summed
            rx1[me, 1:2, cs] = spread
        both = exchange(number, rx1, rx2, True)
        st[0:1, :] = both[0:1] / total
        st[1:2, :] = lax.rsqrt(both[1:2] / total + EPS)

    def norm_silu(ref, st, gain, bias, out):
        mean, scale = st[0:1, :], st[1:2, :]
        steep = scale * gain

        def body(rs, lv, carry):
            z = (ref[rs, :] - mean) * steep + bias
            out[rs, :] = (z * sigmoid(z)).astype(BF)
            return carry

        sweep(body, 0)

    def narrow_cotangent(ref, st, gain, bias, number, place):
        acc = r["acc"]
        mean, scale = st[0:1, :], st[1:2, :]

        def body(rs, lv, carry):
            xhat = (ref[rs, :] - mean) * scale
            z = xhat * gain + bias
            sg = sigmoid(z)
            g = acc[rs, :] * (sg * (1.0 + z * (1.0 - sg)))
            acc[rs, :] = g
            return carry[0] + fold(g), carry[1] + fold(g * xhat)

        zero = jnp.zeros((8, INNER), F32)
        summed, paired = sweep(body, (zero, zero))
        rx1, rx2 = r["rxn1"].at[number], r["rxn2"].at[number]
        rx1[me, 0:1, :] = total_row(summed)
        rx1[me, 1:2, :] = total_row(paired)
        both = exchange(number, rx1, rx2, False)
        r["g_ib"][place : place + 1, :] = both[0:1]
        r["g_ig"][place : place + 1, :] = both[1:2]
        steep = scale * gain
        lift, tilt = both[0:1] / total, both[1:2] / total

        def back(rs, lv, carry):
            xhat = (ref[rs, :] - mean) * scale
            r["dn"][rs, :] = (steep * (acc[rs, :] - lv * (lift + xhat * tilt))).astype(BF)
            return carry

        sweep(back, 0)

    def wide_back(ref, st, gain, both):
        for start in range(0, CHANNELS, 512):
            cs = pl.ds(start, 512)
            mean, scale = st[0:1, cs], st[1:2, cs]
            steep = scale * gain[:, start : start + 512]
            lift = both[0:1, start : start + 512] / total
            tilt = both[1:2, start : start + 512] / total

            def back(rs, lv, carry):
                xhat = (ref[rs, cs] - mean) * scale
                r["dwide"][rs, cs] = (steep * (r["up"][rs, cs] - lv * (lift + xhat * tilt))).astype(BF)
                return carry

            sweep(back, 0)

    def partial_tiles(count, left_of, right, target):
        def step(t, carry):
            slot = lax.rem(t, 2)

            @pl.when(t >= 2)
            def _():
                pltpu.make_async_copy(
                    r["stage"].at[slot], target.at[pl.ds(0, 512)], r["stage_sem"].at[slot]
                ).wait()

            r["stage"][slot] = mm(left_of(t), right[...], TN)
            pltpu.make_async_copy(
                r["stage"].at[slot],
                target.at[pl.ds(pl.multiple_of(t * 512, 512), 512)],
                r["stage_sem"].at[slot],
            ).start()
            return carry

        lax.fori_loop(0, count, step, 0)
        for slot in range(2):
            pltpu.make_async_copy(
                r["stage"].at[slot], target.at[pl.ds(0, 512)], r["stage_sem"].at[slot]
            ).wait()

    def column(ref):
        return lambda t: ref[:, pl.ds(pl.multiple_of(t * 512, 512), 512)]

    def tap(ref, k):
        return ref[pl.ds(pl.multiple_of(k * INNER, INNER), INNER), :]

    def slot_rows(s):
        return pl.ds(s * PIXELS, PIXELS)

    images, between, acc, up = r["images"], r["between"], r["acc"], r["up"]
    stn, stw = r["stn"], r["stw"]
    ig = [r["ig"][i : i + 1, :] for i in range(4)]
    ib = [r["ib"][i : i + 1, :] for i in range(4)]
    bg = [r["bg"][i : i + 1, :] for i in range(2)]
    bb = [r["bb"][i : i + 1, :] for i in range(2)]

    def narrow_stats(ref, number):
        norm_stats(
            ref, INNER, number, r["rxn1"].at[number], r["rxn2"].at[number], stn.at[number]
        )

    def wide_stats(ref, number):
        norm_stats(
            ref, CHANNELS, 8 + number, r["rxw1"].at[number], r["rxw2"].at[number], stw.at[number]
        )

    for s in range(SLOTS):
        level = orient[s]
        q = lax.broadcasted_iota(jnp.int32, (PIXELS, PIXELS), 1)
        p = lax.broadcasted_iota(jnp.int32, (PIXELS, PIXELS), 0)

        def place_of(at):
            long_row = (at >= 36).astype(jnp.int32)
            long_row = long_row + (at >= 72).astype(jnp.int32) + (at >= 108).astype(jnp.int32)
            row = jnp.where(level == 0, long_row, lax.shift_right_logical(at, 2))
            return row, at - row * (LONG - level * (LONG - SHORT))

        row_q, col_q = place_of(q)
        row_p, col_p = place_of(p)
        r["geo"][s, 0] = row_q - row_p
        r["geo"][s, 1] = col_q - col_p

        def hot(k, carry, s=s):
            down = 2 * (k // 3) - 2
            across = 2 * lax.rem(k, 3) - 2
            hit = (r["geo"][s, 0] == down) & (r["geo"][s, 1] == across)
            r["tmat"][s, k] = jnp.where(hit, 1.0, 0.0).astype(BF)
            return carry

        lax.fori_loop(0, TAPS, hot, 0)

    loads["images"].wait()
    loads["red"].wait()
    r["a1"][...] = mm(images[...], r["red"][...], NN)
    pl.semaphore_wait(barrier, dp - 1 + outer - 1)
    narrow_stats(r["a1"], 0)
    norm_silu(r["a1"], stn.at[0], ig[0], ib[0], r["inner"])

    loads["off"].wait()
    inner = r["inner"]
    lane = lax.broadcasted_iota(jnp.int32, (PIXELS, OFFSETS), 1)
    for s in range(SLOTS):
        def gather(k, carry, s=s):
            col = mm(r["tmat"][s, k], inner[slot_rows(s), :], NN).astype(BF)
            return carry + mm(col, tap(r["off"], k), NN)

        offsets = lax.fori_loop(0, TAPS, gather, jnp.zeros((PIXELS, OFFSETS), F32))
        r["frac"][slot_rows(s), :] = sigmoid(offsets)

    def bilinear(s, k):
        down = 2 * (k // 3) - 2
        across = 2 * lax.rem(k, 3) - 2
        frac = r["frac"][slot_rows(s), :]
        fy = jnp.sum(jnp.where(lane == 2 * k, frac, 0.0), axis=1, keepdims=True)
        fx = jnp.sum(jnp.where(lane == 2 * k + 1, frac, 0.0), axis=1, keepdims=True)
        dr, dc = r["geo"][s, 0], r["geo"][s, 1]
        in_y = (dr == down, dr == down + 1)
        in_x = (dc == across, dc == across + 1)
        ay = jnp.where(in_y[0], 1.0 - fy, jnp.where(in_y[1], fy, 0.0))
        ax = jnp.where(in_x[0], 1.0 - fx, jnp.where(in_x[1], fx, 0.0))
        return fy, fx, ay, ax, in_y, in_x

    loads["dfm"].wait()
    acc[...] = jnp.zeros((ROWS, INNER), F32)

    def sample(k, carry):
        for s in range(SLOTS):
            _, _, ay, ax, _, _ = bilinear(s, k)
            weight = (ay * ax).astype(BF)
            r["wmat"][s, k] = weight
            r["samp"][k, slot_rows(s), :] = mm(weight, inner[slot_rows(s), :], NN).astype(BF)
        acc[...] += mm(r["samp"][k], tap(r["dfm"], k), NN)
        return carry

    lax.fori_loop(0, TAPS, sample, 0)
    r["a2"][...] = acc[...]
    narrow_stats(r["a2"], 1)
    norm_silu(r["a2"], stn.at[1], ig[1], ib[1], r["hidden"])

    def widen(source, weight, target):
        def step(n, carry):
            rows = pl.ds(pl.multiple_of(n * 512, 512), 512)
            target[:, rows] = mm(source[...], weight[rows, :], NT)
            return carry

        lax.fori_loop(0, CHANNELS // 512, step, 0)

    loads["exp"].wait()
    widen(r["hidden"], r["exp"], r["a3"])
    wide_stats(r["a3"], 0)
    for start in range(0, CHANNELS, 512):
        cs = pl.ds(start, 512)
        mean = stw[0, 0:1, cs]
        steep = stw[0, 1:2, cs] * bg[0][:, start : start + 512]
        bias = bb[0][:, start : start + 512]

        def join(rs, lv, carry):
            z = (r["a3"][rs, cs] - mean) * steep + bias + images[rs, cs].astype(F32)
            between[rs, cs] = (z * sigmoid(z)).astype(BF)
            return carry

        sweep(join, 0)

    loads["nar"].wait()
    r["b1"][...] = mm(between[...], r["nar"][...], NN)
    narrow_stats(r["b1"], 2)
    norm_silu(r["b1"], stn.at[2], ig[2], ib[2], r["narrow"])

    loads["con"].wait()
    acc[...] = jnp.zeros((ROWS, INNER), F32)

    def convolve(k, carry):
        for s in range(SLOTS):
            r["cols"][k, slot_rows(s), :] = mm(
                r["tmat"][s, k], r["narrow"][slot_rows(s), :], NN
            ).astype(BF)
        acc[...] += mm(r["cols"][k], tap(r["con"], k), NN)
        return carry

    lax.fori_loop(0, TAPS, convolve, 0)
    r["b2"][...] = acc[...]
    narrow_stats(r["b2"], 3)
    norm_silu(r["b2"], stn.at[3], ig[3], ib[3], r["mixed"])

    loads["wid"].wait()
    widen(r["mixed"], r["wid"], r["b3"])
    wide_stats(r["b3"], 1)

    def wide_cotangent(number, ref, st, gain, bias, cotangent):
        rx1, rx2 = r["rxw1"].at[number], r["rxw2"].at[number]
        for start in range(0, CHANNELS, 512):
            cs = pl.ds(start, 512)
            mean, scale = st[0:1, cs], st[1:2, cs]
            gn, bs = gain[:, start : start + 512], bias[:, start : start + 512]

            def body(rs, lv, carry):
                xhat = (ref[rs, cs] - mean) * scale
                g = cotangent(rs, cs, lv, xhat * gn + bs)
                up[rs, cs] = g
                return carry[0] + fold(g), carry[1] + fold(g * xhat)

            zero = jnp.zeros((8, 512), F32)
            summed, paired = sweep(body, (zero, zero))
            rx1[me, 0:1, cs] = total_row(summed)
            rx1[me, 1:2, cs] = total_row(paired)
        return exchange(8 + number, rx1, rx2, False)

    loads["cot"].wait()

    def last(rs, cs, lv, pre):
        z = pre + between[rs, cs].astype(F32)
        sg = sigmoid(z)
        r["obuf"][rs, cs] = (lv * (z * sg)).astype(BF)
        return r["cot"][rs, cs].astype(F32) * (lv * (sg * (1.0 + z * (1.0 - sg))))

    both = wide_cotangent(2, r["b3"], stw.at[1], bg[1], bb[1], last)
    out_copy = pltpu.make_async_copy(r["obuf"], r["out_h"], r["out_sem"].at[0])
    out_copy.start()
    r["g_bb"][1:2, :] = both[0:1]
    r["g_bg"][1:2, :] = both[1:2]
    wide_back(r["b3"], stw.at[1], bg[1], both)

    acc[...] = mm(r["dwide"][...], r["wid"][...], NN)
    narrow_cotangent(r["b2"], stn.at[3], ig[3], ib[3], 4, 3)
    partial_tiles(CHANNELS // 512, column(r["dwide"]), r["mixed"], r["g_wid"])

    acc[...] = jnp.zeros((ROWS, INNER), F32)

    def spread(k, carry):
        for s in range(SLOTS):
            r["turned"][slot_rows(s), :] = mm(
                r["tmat"][s, TAPS - 1 - k], r["dn"][slot_rows(s), :], NN
            ).astype(BF)
        acc[...] += mm(r["turned"][...], tap(r["con"], k), NT)
        return carry

    lax.fori_loop(0, TAPS, spread, 0)
    partial_tiles(TAPS, lambda t: r["cols"][t], r["dn"], r["g_con"])
    narrow_cotangent(r["b1"], stn.at[2], ig[2], ib[2], 5, 2)

    def add_back(n, carry):
        rows = pl.ds(pl.multiple_of(n * 512, 512), 512)
        up[:, rows] += mm(r["dn"][...], r["nar"][rows, :], NT)
        return carry

    lax.fori_loop(0, CHANNELS // 512, add_back, 0)
    partial_tiles(CHANNELS // 512, column(between), r["dn"], r["g_nar"])

    def first(rs, cs, lv, pre):
        z = pre + images[rs, cs].astype(F32)
        sg = sigmoid(z)
        return up[rs, cs] * (sg * (1.0 + z * (1.0 - sg)))

    both = wide_cotangent(3, r["a3"], stw.at[0], bg[0], bb[0], first)
    r["g_bb"][0:1, :] = both[0:1]
    r["g_bg"][0:1, :] = both[1:2]
    wide_back(r["a3"], stw.at[0], bg[0], both)

    acc[...] = mm(r["dwide"][...], r["exp"][...], NN)
    narrow_cotangent(r["a2"], stn.at[1], ig[1], ib[1], 6, 1)
    partial_tiles(CHANNELS // 512, column(r["dwide"]), r["hidden"], r["g_exp"])

    acc[...] = jnp.zeros((ROWS, INNER), F32)
    r["doff"][...] = jnp.zeros((ROWS, OFFSETS), F32)

    def unsample(k, carry):
        r["turned"][...] = mm(r["dn"][...], tap(r["dfm"], k), NT).astype(BF)
        for s in range(SLOTS):
            rs = slot_rows(s)
            grad = r["turned"][rs, :]
            pairs = mm(grad, inner[rs, :], NT)
            fy, fx, ay, ax, in_y, in_x = bilinear(s, k)
            slope_y = jnp.where(in_y[1], ax, 0.0) - jnp.where(in_y[0], ax, 0.0)
            slope_x = jnp.where(in_x[1], ay, 0.0) - jnp.where(in_x[0], ay, 0.0)
            to_y = jnp.sum(pairs * slope_y, axis=1, keepdims=True) * (fy * (1.0 - fy))
            to_x = jnp.sum(pairs * slope_x, axis=1, keepdims=True) * (fx * (1.0 - fx))
            r["doff"][rs, :] += jnp.where(lane == 2 * k, to_y, 0.0) + jnp.where(
                lane == 2 * k + 1, to_x, 0.0
            )
            acc[rs, :] += mm(r["wmat"][s, k], grad, TN)
        return carry

    lax.fori_loop(0, TAPS, unsample, 0)
    partial_tiles(TAPS, lambda t: r["samp"][t], r["dn"], r["g_def"])

    def untap(k, carry):
        columns = pl.ds(pl.multiple_of(k * INNER, INNER), INNER)
        share = jnp.zeros((OFFSETS, INNER), F32)
        for s in range(SLOTS):
            rs = slot_rows(s)
            moved = mm(r["tmat"][s, TAPS - 1 - k], r["doff"][rs, :].astype(BF), NN).astype(BF)
            acc[rs, :] += mm(moved, tap(r["off"], k), NT)
            share = share + mm(moved, inner[rs, :], TN)
        r["ogt"][:, columns] = share
        return carry

    lax.fori_loop(0, TAPS, untap, 0)
    off_copy = pltpu.make_async_copy(r["ogt"], r["g_off"], r["out_sem"].at[1])
    off_copy.start()
    narrow_cotangent(r["a1"], stn.at[0], ig[0], ib[0], 7, 0)

    out_copy.wait()

    def finish(n, carry):
        rows = pl.ds(pl.multiple_of(n * 512, 512), 512)
        r["obuf"][:, rows] = (up[:, rows] + mm(r["dn"][...], r["red"][rows, :], NT)).astype(BF)
        return carry

    lax.fori_loop(0, CHANNELS // 512, finish, 0)
    grad_copy = pltpu.make_async_copy(r["obuf"], r["grad_h"], r["out_sem"].at[2])
    grad_copy.start()
    partial_tiles(CHANNELS // 512, column(images), r["dn"], r["g_red"])
    off_copy.wait()
    grad_copy.wait()
    for count, ref, sem in pending:
        several(count, ref, sem).wait()


def per_device(
    images,
    counts,
    orientation,
    cotangent,
    reducer,
    offseter,
    deformer,
    expander,
    narrower,
    convolver,
    widener,
    inner_gains,
    inner_biases,
    broad_gains,
    broad_biases,
):
    dp, outer = lax.axis_size("dp"), lax.axis_size("outer")
    buffers = scratch(dp, outer)
    names = INPUTS + OUTPUTS + list(buffers)
    smem = pl.BlockSpec(memory_space=pltpu.SMEM)
    vmem = pl.BlockSpec(memory_space=pltpu.VMEM)
    far = pl.BlockSpec(memory_space=pl.ANY)
    shape = jax.ShapeDtypeStruct
    outs = pl.pallas_call(
        functools.partial(kernel, dp, outer, names),
        out_shape=[
            shape((ROWS, CHANNELS), BF),
            shape((ROWS, CHANNELS), BF),
            shape((CHANNELS, INNER), F32),
            shape((OFFSETS, TAPS * INNER), F32),
            shape((TAPS * INNER, INNER), F32),
            shape((CHANNELS, INNER), F32),
            shape((CHANNELS, INNER), F32),
            shape((TAPS * INNER, INNER), F32),
            shape((CHANNELS, INNER), F32),
            shape((4, INNER), F32),
            shape((4, INNER), F32),
            shape((2, CHANNELS), F32),
            shape((2, CHANNELS), F32),
        ],
        in_specs=[smem] * 2 + [vmem] * 4 + [far] * 9,
        out_specs=[far] * 9 + [vmem] * 4,
        scratch_shapes=list(buffers.values()),
        compiler_params=pltpu.CompilerParams(
            collective_id=0, has_side_effects=True, vmem_limit_bytes=60 * 1024 * 1024
        ),
        name="chain",
    )(
        counts,
        orientation,
        inner_gains,
        inner_biases,
        broad_gains,
        broad_biases,
        images.reshape(ROWS, CHANNELS),
        cotangent.reshape(ROWS, CHANNELS),
        reducer,
        offseter,
        deformer,
        expander,
        narrower,
        convolver,
        widener,
    )
    out, grad, g_red, g_off, g_def, g_exp, g_nar, g_con, g_wid, g_ig, g_ib, g_bg, g_bb = outs
    parts = [
        lax.psum_scatter(part, "dp", scatter_dimension=0, tiled=True)
        for part in (g_red, g_off.T, g_def, g_exp, g_nar, g_con, g_wid)
    ]
    parts = lax.psum(parts, "outer")
    place = lax.axis_index("dp")
    inner_share, broad_share = INNER // dp, CHANNELS // dp
    return (
        out.reshape(SLOTS, PIXELS, CHANNELS),
        grad.reshape(SLOTS, PIXELS, CHANNELS),
        *parts,
        lax.dynamic_slice_in_dim(g_ig, place * inner_share, inner_share, 1),
        lax.dynamic_slice_in_dim(g_ib, place * inner_share, inner_share, 1),
        lax.dynamic_slice_in_dim(g_bg, place * broad_share, broad_share, 1),
        lax.dynamic_slice_in_dim(g_bb, place * broad_share, broad_share, 1),
    )


def solution(mesh):
    spread = P(("dp", "outer"), None, None)
    in_specs = (spread, P(), P(("dp", "outer")), spread) + (P(),) * 11
    out_specs = (spread, spread) + (P("dp", None),) * 7 + (P(None, "dp"),) * 4
    return jax.shard_map(
        per_device, mesh=mesh, in_specs=in_specs, out_specs=out_specs, check_vma=False
    )
```

time: 1790 us -> 783 us (0.44)
  blocking collectives: 748 us -> 21.7 us
  local copies, waits for them, and re-layouts: 350 us -> 16.1 us
  other arithmetic: 202 us -> 0 us
  waiting for transfers between devices: 373 us -> 562 us
  Pallas kernels: 0 us -> 168 us
  matrix products: 83.4 us -> 0 us
    psum x19 -> x1, blocking collectives: 748 us -> 21.7 us  [per_device(): parts = lax.psum(parts, 'outer')]
    gather x32 -> x0, local copies, waits for them, and re-layouts: 244 us -> none  [the longest x8 134 us: spread_taps(): taken = blocks[index, jnp.arange(TAPS, dtype=jnp.int32)[None, :]]]
    reduce_scatter x6, waiting for transfers between devices: 187 us -> 370 us  [per_device(): lax.psum_scatter(part, 'dp', scatter_dimension=0, tiled=True)]
    pallas_call x0 -> x1, Pallas kernels: none -> 168 us  [per_device(): pl.pallas_call(functools.partial(kernel, dp, outer, names), out_shape=[sh...]
    scatter-add x8 -> x0, other arithmetic: 83.5 us -> none  [sample(): total = total + weight[:, :, None] * field[index]]
    dot_general x22 -> x0, matrix products: 80.7 us -> none  [the longest x1 7.27 us: per_device(): lax.dot_general(columns_two, back_e, ROWS_TOGETHER, preferred_element_typ...]
    reduce_sum x16 -> x0, other arithmetic: 56.8 us -> none  [the longest x2 33.3 us: sample(): total = total + weight[:, :, None] * field[index]]
    mul x19 -> x0, local copies, waits for them, and re-layouts: 47.4 us -> none  [the longest x16 39.6 us: sample(): total = total + weight[:, :, None] * field[index]]
  transfers between devices with their start and end apart: 8 -> 8, of which waited for: 5 -> 8; matrix products, arithmetic and copies ran while one was open for 22% -> 1% of each run, Pallas kernels for 0% -> 0%
where the time goes in v1:
time: 783 us
  waiting for transfers between devices  562 us (72%)
  Pallas kernels  168 us (21%)
  blocking collectives  21.7 us (3%)
  local copies, waits for them, and re-layouts  16.1 us (2%)
  between operations  14.2 us (2%)
    reduce_scatter x6, waiting for transfers between devices, per_device(): lax.psum_scatter(part, 'dp', scatter_dimension=0, tiled=True)  370 us
    pallas_call x1, Pallas kernels, per_device(): pl.pallas_call(functools.partial(kernel, dp, outer, names), out_shape=[sh...  168 us
    psum x1, waiting for transfers between devices, per_device(): parts = lax.psum(parts, 'outer')  146 us
    unnamed x9, waiting for transfers between devices  46.1 us
    psum x1, blocking collectives, per_device(): parts = lax.psum(parts, 'outer')  21.7 us
  transfers between devices with their start and end apart: 8, of which 8 were waited for; matrix products, arithmetic and copies ran while one was open for 1% of the time, Pallas kernels for 0%

profile of v1, /device:TPU:0, one launch (start us, length us, event | category | flops | bytes accessed | tf_op | source)
XLA Modules:
  0.0 782.6 jit_solution(14582878952472555367)
XLA Ops:
  7.2 2.4 copy.29.refs_9_
  9.6 168.0 %chain.1 = (bf16[288,2048]{1,0:T(8,128)(2,1)}, bf16[288,2048]{1,0:T(8,128)(2,1)}, f32[2048,512]{1,0:T(8,128)}, f32[18,4608]{1,0:T(8,128)}, f32[4608,512]{1,0:T(8...) custom-call(s32[32]{0:T(128)} %refs_0_.1, ...), custom_call_target="tpu_custom_call" | custom-call | tf_op jit(solution)/shard_map/chain/pallas_call | solution.py:637
  177.7 0.7 reduce-scatter.14.cloned.1.call-update
  181.3 2.2 copy.30
  183.6 45.4 %reduce-scatter.10.cloned.1.call-done = f32[256,512]{1,0:T(8,128)} async-done(((f32[2048,512]{1,0:T(8,128)}), f32[256,512]{1,0:T(8,128)}) %reduce-scatter.10.cloned.1.call-update) | async-done | bytes 524304 | tf_op jit(solution)/shard_map/reduce_scatter | solution.py:680
  229.0 55.1 %reduce-scatter.14.cloned.1.call-done = f32[256,512]{1,0:T(8,128)} async-done(((f32[2048,512]{1,0:T(8,128)}), f32[256,512]{1,0:T(8,128)}) %reduce-scatter.14.cloned.1.call-update) | async-done | bytes 524304 | tf_op jit(solution)/shard_map/reduce_scatter | solution.py:680
  284.0 54.7 %reduce-scatter.16.cloned.1.call-done = f32[256,512]{1,0:T(8,128)} async-done(((f32[2048,512]{1,0:T(8,128)}), f32[256,512]{1,0:T(8,128)}) %reduce-scatter.16.cloned.1.call-update) | async-done | bytes 524304 | tf_op jit(solution)/shard_map/reduce_scatter | solution.py:680
  338.8 54.9 %reduce-scatter.20.cloned.1.call-done = f32[256,512]{1,0:T(8,128)} async-done(((f32[2048,512]{1,0:T(8,128)}), f32[256,512]{1,0:T(8,128)}) %reduce-scatter.20.cloned.1.call-update) | async-done | bytes 524304 | tf_op jit(solution)/shard_map/reduce_scatter | solution.py:680
  393.7 79.9 %reduce-scatter.12.cloned.1.call-done = f32[576,512]{1,0:T(8,128)} async-done(((f32[4608,512]{1,0:T(8,128)}), f32[576,512]{1,0:T(8,128)}) %reduce-scatter.12.cloned.1.call-update) | async-done | bytes 1179664 | tf_op jit(solution)/shard_map/reduce_scatter | solution.py:680
  473.6 79.9 %reduce-scatter.18.cloned.1.call-done = f32[576,512]{1,0:T(8,128)} async-done(((f32[4608,512]{1,0:T(8,128)}), f32[576,512]{1,0:T(8,128)}) %reduce-scatter.18.cloned.1.call-update) | async-done | bytes 1179664 | tf_op jit(solution)/shard_map/reduce_scatter | solution.py:680
  553.5 1.4 constant_dynamic-slice_fusion
  554.9 1.3 constant_dynamic-slice_fusion.2
  556.2 43.1 %reduce-scatter.22.cloned.1.call-done = f32[576,18]{1,0:T(8,128)} async-done(((f32[4608,18]{1,0:T(8,128)}), f32[576,18]{1,0:T(8,128)}) %reduce-scatter.22.cloned.1.call-update) | async-done | bytes 41488
  599.3 1.1 copy.31
  600.4 21.7 %psum.50 = f32[576,18]{0,1:T(8,128)} all-reduce(f32[576,18]{0,1:T(8,128)S(1)} %copy.31), channel_id=1, replica_groups=mesh['dp'=8,'outer'=4] {'outer'}, use_global_device_ids=true, to_apply=%region_3.0 | all-reduce | flops 10368 | bytes 82944 | tf_op jit(solution)/shard_map/psum | solution.py:683
  622.1 146.4 %all-reduce.3.cloned.1.call-done = (f32[256,512]{1,0:T(8,128)}, f32[576,512]{1,0:T(8,128)}, f32[256,512]{1,0:T(8,128)}, f32[256,512]{1,0:T(8,128)}, f32[576,512]{1,0:T(8,128)}, /*index=5*/f32[256,512]{1,0:T(8,128)}) async-done(((f32[256,512]{1,0:T(8,128)}, f32[576,512]{1,0:T(8,128)}, f32[256,512]{1,0:T(8,128)}, f32[256,512]{1,0:T(8,128)}, f32[576,512]{1,0:T(8,128)}, /*index=5*/f32[256,512]{1,0:T(8,128)}), ...) | async-done | bytes 4456464 | tf_op jit(solution)/shard_map/psum | solution.py:683
  768.5 1.0 copy.40
  769.6 1.0 copy.41
  770.6 0.8 copy.42
  771.4 1.0 copy.43
  772.4 0.8 copy.44
  773.2 0.8 copy.45
  774.0 1.0 copy.46
  775.0 0.8 copy.47
  (33 shorter events, 3.1 us)
Async XLA Ops:
  7.2 221.8 %reduce-scatter.10.cloned.1.call-start = ((), (), s32[]{:S(2)}) async-start(), calls=%async_computation.7 | async-start | bytes 4718592 | tf_op jit(solution)/shard_map/reduce_scatter | solution.py:680
  177.6 106.4 %reduce-scatter.14.cloned.1.call-start = ((), (), s32[]{:S(2)}) async-start(), calls=%async_computation.9 | async-start | bytes 4718592 | tf_op jit(solution)/shard_map/reduce_scatter | solution.py:680
  178.4 160.4 %reduce-scatter.16.cloned.1.call-start = ((), (), s32[]{:S(2)}) async-start(), calls=%async_computation.10 | async-start | bytes 4718592 | tf_op jit(solution)/shard_map/reduce_scatter | solution.py:680
  179.1 214.6 %reduce-scatter.20.cloned.1.call-start = ((), (), s32[]{:S(2)}) async-start(), calls=%async_computation.12 | async-start | bytes 4718592 | tf_op jit(solution)/shard_map/reduce_scatter | solution.py:680
  179.7 293.9 %reduce-scatter.12.cloned.1.call-start = ((), (), s32[]{:S(2)}) async-start(), calls=%async_computation.8 | async-start | bytes 10616832 | tf_op jit(solution)/shard_map/reduce_scatter | solution.py:680
  180.3 373.2 %reduce-scatter.18.cloned.1.call-start = ((), (), s32[]{:S(2)}) async-start(), calls=%async_computation.11 | async-start | bytes 10616832 | tf_op jit(solution)/shard_map/reduce_scatter | solution.py:680
  180.3 1.0 copy-start.8
  180.8 418.5 %reduce-scatter.22.cloned.1.call-start = ((), (), s32[]{:S(2)}) async-start(), calls=%async_computation.13 | async-start | bytes 2654208
  183.5 585.0 %all-reduce.3.cloned.1.call-start = ((), (), s32[]{:S(2)}) async-start(), calls=%async_computation.14 | async-start | bytes 8912896 | tf_op jit(solution)/shard_map/psum | solution.py:683
  553.5 215.1 %copy-start.1 = (bf16[288,2048]{1,0:T(8,128)(2,1)S(1)}, bf16[288,2048]{1,0:T(8,128)(2,1)}, u32[]{:S(2)}) copy-start(bf16[288,2048]{1,0:T(8,128)(2,1)} %get-tuple-element.26) | copy-start | bytes 3538948
  553.5 216.1 %copy-start = (bf16[288,2048]{1,0:T(8,128)(2,1)S(1)}, bf16[288,2048]{1,0:T(8,128)(2,1)}, u32[]{:S(2)}) copy-start(bf16[288,2048]{1,0:T(8,128)(2,1)} %get-tuple-element.27) | copy-start | bytes 3538948
  768.5 2.0 copy-start.7
  769.6 1.8 copy-start.3
  770.6 1.8 copy-start.6
  770.6 2.6 copy-start.5
  771.4 2.6 copy-start.2
  772.4 2.6 copy-start.4
Sparse Core Ops, SparseCore 0:
  177.7 51.1 reduce-scatter.9
  232.7 51.3 reduce-scatter.13
  287.4 51.3 reduce-scatter.15
  342.3 51.3 reduce-scatter.19
  397.1 76.4 reduce-scatter.11
  476.9 76.4 reduce-scatter.17
  556.8 42.4 reduce-scatter.21
  602.4 166.1 all-reduce.2

commit v2 on v1

v2 whole, which is shorter than its diff:
```python
import functools
import math
import types

import jax
import jax.numpy as jnp
from jax import lax
from jax.experimental import pallas as pl
from jax.experimental.pallas import tpu as pltpu
from jax.sharding import PartitionSpec as P

CHANNELS = 2048
INNER = 512
TAPS = 9
SLOTS = 2
SHORT = 4
LONG = 36
PIXELS = 144
ROWS = SLOTS * PIXELS
OFFSETS = 2 * TAPS
EPS = 1e-05
BF = jnp.bfloat16
F32 = jnp.float32
MESH = pl.DeviceIdType.MESH
NN = (((1,), (0,)), ((), ()))
NT = (((1,), (1,)), ((), ()))
TN = (((0,), (0,)), ((), ()))


def mm(left, right, dims):
    return lax.dot_general(left, right, dims, preferred_element_type=F32)


def sigmoid(value):
    return 0.5 * jnp.tanh(0.5 * value) + 0.5


def fold(value):
    return jnp.sum(value.reshape(value.shape[0] // 8, 8, value.shape[1]), axis=0)


def total_row(value):
    return jnp.sum(value, axis=0, keepdims=True)


def layout(dp):
    chips = dp // 2
    bits = chips.bit_length() - 1
    wide = CHANNELS // dp
    deep = TAPS * INNER // dp
    taps = max(
        -(-(2 * deep * chip % INNER + 2 * deep) // INNER) for chip in range(chips)
    )
    return chips, bits, wide, deep, taps


def scratch(dp, outer):
    vmem = pltpu.VMEM
    dma = pltpu.SemaphoreType.DMA
    chips, bits, wide, deep, taps = layout(dp)
    everyone = dp * outer
    group = min(chips, 4)
    return dict(
        images=vmem((ROWS, CHANNELS), BF),
        between=vmem((ROWS, CHANNELS), BF),
        dwide=vmem((ROWS, CHANNELS), BF),
        obuf=vmem((ROWS, CHANNELS), BF),
        redwid=vmem((CHANNELS, INNER), BF),
        exp=vmem((CHANNELS, INNER), BF),
        nar=vmem((CHANNELS, INNER), BF),
        dfmcon=vmem((TAPS * INNER, INNER), BF),
        off=vmem((TAPS * INNER, OFFSETS), BF),
        a1=vmem((ROWS, INNER), F32),
        a2=vmem((ROWS, INNER), F32),
        b1=vmem((ROWS, INNER), F32),
        b2=vmem((ROWS, INNER), F32),
        acc=vmem((ROWS, INNER), F32),
        a3=vmem((CHANNELS // 512, ROWS, 512), F32),
        b3=vmem((CHANNELS // 512, ROWS, 512), F32),
        up=vmem((CHANNELS // 512, ROWS, 512), F32),
        inner=vmem((ROWS, INNER), BF),
        hidden=vmem((ROWS, INNER), BF),
        narrow=vmem((ROWS, INNER), BF),
        mixed=vmem((ROWS, INNER), BF),
        dn=vmem((ROWS, INNER), BF),
        turned=vmem((ROWS, INNER), BF),
        wmat=vmem((SLOTS, TAPS, PIXELS, PIXELS), BF),
        tmat=vmem((2, TAPS, PIXELS, PIXELS), BF),
        geo=vmem((2, 2, PIXELS, PIXELS), jnp.int32),
        frac=vmem((ROWS, OFFSETS), F32),
        doff=vmem((ROWS, OFFSETS), F32),
        stn=vmem((4, 2, INNER), F32),
        stw=vmem((2, 2, CHANNELS), F32),
        rxn=vmem((8, everyone, 2, INNER), F32),
        rxw1=vmem((4, dp, 2, CHANNELS), F32),
        rxw2=vmem((4, outer, 2, CHANNELS), F32),
        pool=vmem((3, chips, wide, INNER), F32),
        corel=vmem((chips, wide, INNER), F32),
        land=vmem((2, 2, chips - 1, wide, INNER // 2), F32),
        zwide=vmem((2, 3, wide, INNER), F32),
        tiny=vmem((2, chips, SLOTS, 24, PIXELS), F32),
        give=vmem((ROWS, INNER), F32),
        taken=vmem((group, ROWS, INNER), F32),
        drawn=vmem((2, ROWS, INNER), F32),
        yall=vmem((group * ROWS, INNER), BF),
        xall=vmem((group * ROWS, INNER), BF),
        grad=vmem((taps * INNER, INNER), F32),
        cored=vmem((deep, INNER), F32),
        zdeep=vmem((2, 2, deep // 2, INNER), F32),
        goff=vmem((24, taps * INNER), F32),
        coreo=vmem((24, taps * INNER), F32),
        zoff=vmem((2, 24, taps * INNER), F32),
        free=pltpu.SemaphoreType.REGULAR,
        load_sem=dma((11,)),
        out_sem=dma((2,)),
        res_sem=dma((7, 2)),
        xn_s=dma((8,)),
        xn_r=dma((8,)),
        xw_s=dma((4, 2)),
        xw_r=dma((4, 2)),
        core_s=dma((7,)),
        core_r=dma((7,)),
        step_s=dma((4, 2, bits)),
        step_r=dma((4, 2, bits)),
        give_sem=dma((4,)),
        take_sem=dma((3,)),
        ag_s=dma((4, 2, bits)),
        ag_r=dma((4, 2, bits)),
        tiny_s=dma((2,)),
        tiny_r=dma((2,)),
        z_s=dma((7, 2, 3)),
        z_r=dma((7, 2, 3)),
    )


def kernel(dp, outer, names, *refs):
    assert outer == 4
    r = types.SimpleNamespace(**dict(zip(names, refs)))
    chips, bits, wide, deep, taps = layout(dp)
    everyone = dp * outer
    me = lax.axis_index("dp")
    mine = lax.axis_index("outer")
    own = me * outer + mine
    core = lax.rem(me, 2)
    chip = lax.div(me, 2)
    sibling = (me + 1 - 2 * core, mine)
    inside = (mine == 1) | (mine == 2)
    outside = (mine == 0) | (mine == 3)
    counts, orient = r.counts, r.orient
    dma = pltpu.make_async_copy

    loads = types.SimpleNamespace()

    def load(place, source, target):
        copy = dma(source, target, r.load_sem.at[place])
        copy.start()
        return copy

    loads.images_h = load(0, r.images_h, r.images)
    loads.red_h = load(1, r.red_h, r.redwid)
    loads.off_h = load(2, r.off_h, r.off)
    loads.def_h = load(3, r.def_h, r.dfmcon)
    loads.exp_h = load(4, r.exp_h, r.exp)
    loads.nar_h = load(5, r.nar_h, r.nar)
    loads.cot_h = load(6, r.cot_h, r.dwide)

    def other(step):
        target = lax.rem(own + step, everyone)
        return lax.div(target, outer), lax.rem(target, outer)

    barrier = pltpu.get_barrier_semaphore()

    def greet(step, carry):
        pl.semaphore_signal(barrier, inc=1, device_id=other(step), device_id_type=MESH)
        return carry

    lax.fori_loop(1, everyone, greet, 0)

    def size(i, carry):
        sizes, near, far = carry
        row, place = lax.div(i, outer), lax.rem(i, outer)
        held = counts[i].astype(F32)
        here = jnp.where(place == mine, held, 0.0)

        def mark(count, at, value):
            line = lax.broadcasted_iota(jnp.int32, (count, 1), 0)
            return jnp.where(line == at, value, 0.0)

        return (
            sizes + mark(everyone, i, held),
            near + mark(dp, row, here),
            far + mark(outer, place, held),
        )

    zeros = tuple(jnp.zeros((count, 1), F32) for count in (everyone, dp, outer))
    sizes, near, far = (
        value * float(PIXELS) for value in lax.fori_loop(0, everyone, size, zeros)
    )
    near_total = total_row(near)
    total = total_row(far)
    held = counts[own].astype(F32)
    live1 = held - 1.0
    local = held * float(PIXELS)

    def sweep(body, init):
        def step(i, carry):
            lv = jnp.where(i < 3, 1.0, live1)
            for j in range(3):
                carry = body(pl.ds(pl.multiple_of(i * 48 + j * 16, 16), 16), lv, carry)
            return carry

        return lax.fori_loop(0, 6, step, init)

    def send(source, target, sent, received, device):
        pltpu.make_async_remote_copy(
            src_ref=source,
            dst_ref=target,
            send_sem=sent,
            recv_sem=received,
            device_id=device,
            device_id_type=MESH,
        ).start()

    def settle(view, sem):
        dma(view, view, sem).wait()

    waiting = {}

    def later(tag, view, sem, when=None):
        waiting.setdefault(tag, []).append((when, view, sem))

    def flush(tag):
        for when, view, sem in waiting.pop(tag, []):
            if when is None:
                settle(view, sem)
            else:
                pl.when(when)(functools.partial(settle, view, sem))

    def accumulate(target, source):
        rows = target.shape[0]
        step = math.gcd(rows, 32)

        def body(i, carry):
            rs = pl.ds(pl.multiple_of(i * step, 8), step)
            target[rs, :] += source[rs, :]
            return carry

        lax.fori_loop(0, rows // step, body, 0)

    def mix(target, one, two):
        rows = target.shape[0]
        step = math.gcd(rows, 32)

        def body(i, carry):
            rs = pl.ds(pl.multiple_of(i * step, 8), step)
            target[rs, :] = one[rs, :] + two[rs, :]
            return carry

        lax.fori_loop(0, rows // step, body, 0)

    def flip(value, bit):
        weight = 1 << bit
        return value + weight - 2 * weight * lax.rem(lax.div(value, weight), 2)

    def bit_of(value, bit):
        return lax.rem(lax.div(value, 1 << bit), 2)

    orders = [
        list(range(bits)),
        list(range(bits // 2, bits)) + list(range(bits // 2)),
    ]
    halves = [pl.ds(0, INNER // 2), pl.ds(INNER // 2, INNER // 2)]

    def merge(rx, counted, size, forward):
        first = rx[:, 0, :]
        second = rx[:, 1, :]
        if forward:
            summed = total_row(first)
            apart = first / counted - summed / size
            spread = total_row(second + counted * apart * apart)
            return jnp.concatenate([summed, spread], axis=0)
        return jnp.concatenate([total_row(first), total_row(second)], axis=0)

    def nothing():
        pass

    def share_narrow(number, forward, work):
        rx = r.rxn.at[number]

        def step(i, carry):
            send(rx.at[own], rx.at[own], r.xn_s.at[number], r.xn_r.at[number], other(i))
            return carry

        lax.fori_loop(1, everyone, step, 0)
        rest = rx.at[pl.ds(0, everyone - 1)]
        later("end", rest, r.xn_s.at[number])
        work()
        settle(rest, r.xn_r.at[number])
        return merge(rx, sizes, total, forward)

    def share_wide(number, forward, work, work_more):
        rx1, rx2 = r.rxw1.at[number], r.rxw2.at[number]
        for step in range(1, dp):
            send(
                rx1.at[me],
                rx1.at[me],
                r.xw_s.at[number, 0],
                r.xw_r.at[number, 0],
                (lax.rem(me + step, dp), mine),
            )
        rest = rx1.at[pl.ds(0, dp - 1)]
        later("end", rest, r.xw_s.at[number, 0])
        work()
        settle(rest, r.xw_r.at[number, 0])
        rx2[mine] = merge(rx1, near, near_total, forward)
        for step in range(1, outer):
            send(
                rx2.at[mine],
                rx2.at[mine],
                r.xw_s.at[number, 1],
                r.xw_r.at[number, 1],
                (me, lax.rem(mine + step, outer)),
            )
        rest = rx2.at[pl.ds(0, outer - 1)]
        later("end", rest, r.xw_s.at[number, 1])
        work_more()
        settle(rest, r.xw_r.at[number, 1])
        return merge(rx2, far, total, forward)

    def local_stats(ref, put, cs):
        zero = jnp.zeros((8, 512), F32)
        summed = total_row(sweep(lambda rs, lv, c: c + lv * fold(ref[rs, :]), zero))
        mean = summed / local

        def squares(rs, lv, carry):
            apart = ref[rs, :] - mean
            return carry + lv * fold(apart * apart)

        put[0:1, cs] = summed
        put[1:2, cs] = total_row(sweep(squares, zero))

    def keep_stats(both, st):
        st[0:1, :] = both[0:1] / total
        st[1:2, :] = lax.rsqrt(both[1:2] / total + EPS)

    def narrow_stats(ref, number, work=nothing):
        local_stats(ref, r.rxn.at[number, own], pl.ds(0, INNER))
        keep_stats(share_narrow(number, True, work), r.stn.at[number])

    blocks = [pl.ds(start, 512) for start in range(0, CHANNELS, 512)]

    def wide_stats(ref, number, work=nothing, work_more=nothing):
        for n, cs in enumerate(blocks):
            local_stats(ref.at[n], r.rxw1.at[number, me], cs)
        keep_stats(share_wide(number, True, work, work_more), r.stw.at[number])

    def norm_silu(ref, number, gain, bias, out, spread):
        st = r.stn.at[number]
        mean, scale = st[0:1, :], st[1:2, :]
        steep = scale * gain

        def body(rs, lv, carry):
            z = (ref[rs, :] - mean) * steep + bias
            value = (z * sigmoid(z)).astype(BF)
            out[rs, :] = value
            if spread:
                r.give[rs, :] = value.astype(F32)
            return carry

        sweep(body, 0)

    def narrow_cotangent(ref, place, gain, bias, number, spread, work=nothing):
        acc = r.acc
        st = r.stn.at[place]
        mean, scale = st[0:1, :], st[1:2, :]

        def body(rs, lv, carry):
            xhat = (ref[rs, :] - mean) * scale
            z = xhat * gain + bias
            sg = sigmoid(z)
            g = acc[rs, :] * (sg * (1.0 + z * (1.0 - sg)))
            acc[rs, :] = g
            return carry[0] + fold(g), carry[1] + fold(g * xhat)

        zero = jnp.zeros((8, INNER), F32)
        summed, paired = sweep(body, (zero, zero))
        put = r.rxn.at[number, own]
        put[0:1, :] = total_row(summed)
        put[1:2, :] = total_row(paired)
        both = share_narrow(number, False, work)
        r.g_ib[place : place + 1, :] = both[0:1]
        r.g_ig[place : place + 1, :] = both[1:2]
        steep = scale * gain
        lift, tilt = both[0:1] / total, both[1:2] / total

        def back(rs, lv, carry):
            xhat = (ref[rs, :] - mean) * scale
            value = (steep * (acc[rs, :] - lv * (lift + xhat * tilt))).astype(BF)
            r.dn[rs, :] = value
            if spread:
                r.give[rs, :] = value.astype(F32)
            return carry

        sweep(back, 0)

    def wide_cotangent(number, ref, place, gain, bias, cotangent, work=nothing, work_more=nothing):
        put = r.rxw1.at[number, me]
        st = r.stw.at[place]
        for n, cs in enumerate(blocks):
            mean, scale = st[0:1, cs], st[1:2, cs]
            gn, bs = gain[:, 512 * n : 512 * n + 512], bias[:, 512 * n : 512 * n + 512]

            def body(rs, lv, carry):
                xhat = (ref[n, rs, :] - mean) * scale
                g = cotangent(n, rs, cs, lv, xhat * gn + bs)
                r.up[n, rs, :] = g
                return carry[0] + fold(g), carry[1] + fold(g * xhat)

            zero = jnp.zeros((8, 512), F32)
            summed, paired = sweep(body, (zero, zero))
            put[0:1, cs] = total_row(summed)
            put[1:2, cs] = total_row(paired)
        both = share_wide(number, False, work, work_more)
        r.g_bb[place : place + 1, :] = both[0:1]
        r.g_bg[place : place + 1, :] = both[1:2]
        for n, cs in enumerate(blocks):
            mean, scale = st[0:1, cs], st[1:2, cs]
            span = slice(512 * n, 512 * n + 512)
            steep = scale * gain[:, span]
            lift, tilt = both[0:1, span] / total, both[1:2, span] / total

            def back(rs, lv, carry):
                xhat = (ref[n, rs, :] - mean) * scale
                value = steep * (r.up[n, rs, :] - lv * (lift + xhat * tilt))
                r.dwide[rs, cs] = value.astype(BF)
                return carry

            sweep(back, 0)

    def tap(ref, k):
        return ref[pl.ds(pl.multiple_of(k * INNER, INNER), INNER), :]

    def slot_rows(s):
        return pl.ds(s * PIXELS, PIXELS)

    def steps_of(k):
        return 2 * lax.div(k, 3) - 2, 2 * lax.rem(k, 3) - 2

    WID, CON, NAR, EXP, DEF, RED, OFF = range(7)
    nth = {WID: 0, NAR: 1, EXP: 2, RED: 3}
    result = {
        WID: r.g_wid,
        CON: r.g_con,
        NAR: r.g_nar,
        EXP: r.g_exp,
        DEF: r.g_def,
        RED: r.g_red,
        OFF: r.g_off,
    }
    pool, land, grad, far_blocks = r.pool, r.land, r.grad, r.far_blocks

    def z_parts(u):
        if u in nth:
            if u == RED:
                hold = [r.a3.at[i, pl.ds(0, wide)] for i in range(3)]
            else:
                hold = [r.zwide.at[nth[u] % 2, i] for i in range(3)]
            for hs in halves:
                yield tuple(ref.at[:, hs] for ref in hold) + (result[u].at[:, hs],)
        elif u == OFF:
            yield r.goff, r.zoff.at[0], r.zoff.at[1], result[u]
        else:
            for q in range(2):
                source = r.b3.at[(2 if u == DEF else 0) + q]
                if u == DEF:
                    first, second = (r.b1, r.a2) if q == 0 else (r.b2, r.a3.at[3])
                else:
                    first, second = r.zdeep.at[0, q], r.zdeep.at[1, q]
                rows = pl.ds(0, deep // 2)
                out = result[u].at[pl.ds(q * (deep // 2), deep // 2)]
                yield source.at[rows], first.at[rows], second.at[rows], out

    def z_sems(u, q, step):
        return r.z_s.at[u, q, step], r.z_r.at[u, q, step]

    def z1(u):
        for q, (source, first, second, out) in enumerate(z_parts(u)):
            sent, received = z_sems(u, q, 0)

            @pl.when(outside)
            def _():
                send(source, first, sent, received, (me, flip(mine, 0)))

            later(("z", u), source, sent, outside)

    def z2(u):
        for q, (source, first, second, out) in enumerate(z_parts(u)):
            sent, received = z_sems(u, q, 1)

            @pl.when(inside)
            def _():
                settle(first, z_sems(u, q, 0)[1])
                accumulate(source, first)
                send(source, second, sent, received, (me, 3 - mine))

            later(("z", u), source, sent, inside)

    def z3(u):
        for q, (source, first, second, out) in enumerate(z_parts(u)):
            sent, received = z_sems(u, q, 2)

            @pl.when(inside)
            def _():
                settle(second, z_sems(u, q, 1)[1])
                accumulate(second, source)
                send(second, first, sent, received, (me, flip(mine, 0)))
                dma(second, out, r.res_sem.at[u, q]).start()

            later(("zl", u), second, sent, inside)

    def z4(u):
        for q, (source, first, second, out) in enumerate(z_parts(u)):

            @pl.when(outside)
            def _():
                settle(first, z_sems(u, q, 2)[1])
                dma(first, out, r.res_sem.at[u, q]).start()

    def z_clear(u):
        flush(("z", u))
        flush(("zl", u))
        for q, (source, first, second, out) in enumerate(z_parts(u)):
            dma(first, out, r.res_sem.at[u, q]).wait()

    def wide_begin(u, left, right):
        p = nth[u] % 2
        flush("sib")
        flush(("keep", p))
        low = p + (2 - p) * core
        high = p + (2 - p) * (1 - core)

        def step(m, carry):
            block = left[:, pl.ds(pl.multiple_of(m * (2 * wide), 2 * wide), 2 * wide)]
            pool[low, m] = mm(block[:, :wide], right[...], TN)
            pool[high, m] = mm(block[:, wide:], right[...], TN)
            send(
                pool.at[2, m], r.corel.at[m], r.core_s.at[u], r.core_r.at[u], sibling
            )
            return carry

        lax.fori_loop(0, chips, step, 0)
        later("sib", r.corel, r.core_s.at[u])

    def piece(h, t, j, toward):
        value = 0
        for i, bit in enumerate(orders[h]):
            if i < t:
                part = bit_of(chip, bit)
            elif i == t:
                part = bit_of(toward, bit)
            else:
                part = (j >> (i - t - 1)) & 1
            value = value + part * (1 << bit)
        return value

    def step_place(u, h, t):
        first, count = chips - (chips >> t), chips >> (t + 1)
        p = nth[u] % 2
        sems = r.step_s.at[nth[u], h, t], r.step_r.at[nth[u], h, t]
        return p, first, count, sems, land.at[p, h, pl.ds(first, count)]

    def wide_send(u, t):
        for h in range(2):
            p, first, count, (sent, received), region = step_place(u, h, t)
            toward = flip(chip, orders[h][t])
            for j in range(count):
                send(
                    pool.at[p, piece(h, t, j, toward), :, halves[h]],
                    land.at[p, h, first + j],
                    sent,
                    received,
                    (2 * toward + core, mine),
                )
            later(("keep", p), region, sent)

    def wide_add(u, t):
        for h in range(2):
            p, first, count, (sent, received), region = step_place(u, h, t)
            settle(region, received)
            if t == bits - 1:
                mix(list(z_parts(u))[h][0], pool.at[p, chip, :, halves[h]], land.at[p, h, first])
                continue
            for j in range(count):
                accumulate(
                    pool.at[p, piece(h, t, j, chip), :, halves[h]], land.at[p, h, first + j]
                )

    def wide_core(u):
        p = nth[u] % 2
        settle(r.corel, r.core_r.at[u])

        def step(m, carry):
            accumulate(pool.at[p, m], r.corel.at[m])
            return carry

        lax.fori_loop(0, chips, step, 0)
        wide_send(u, 0)

    def wide_step(u, t):
        wide_add(u, t - 1)
        if t < bits:
            wide_send(u, t)
        else:
            z1(u)

    def held_at(h, j):
        value = chip
        for i in range(bits):
            if (j >> i) & 1:
                value = flip(value, orders[h][i])
        return value

    def gather_send(a, t):
        for h in range(2):
            partner = flip(chip, orders[h][t])
            sent, received = r.ag_s.at[a, h, t], r.ag_r.at[a, h, t]
            for j in range(1 << t):
                block = far_blocks.at[a, held_at(h, j), :, halves[h]]
                source = r.give.at[:, halves[h]] if j == 0 else block
                send(source, block, sent, received, (2 * partner + core, mine))
            later(("ag", a), far_blocks.at[a, pl.ds(0, 1 << t), :, halves[h]], sent)

    def gather_start(a):
        block = far_blocks.at[a, chip]
        dma(r.give, block, r.give_sem.at[a]).start()
        later(("ag", a), block, r.give_sem.at[a])
        gather_send(a, 0)

    def gather_wait(a, t):
        for h in range(2):
            settle(far_blocks.at[a, pl.ds(0, 1 << t), :, halves[h]], r.ag_r.at[a, h, t])

    def gather_step(a, t):
        gather_wait(a, t - 1)
        gather_send(a, t)

    def gather_end(a):
        gather_wait(a, bits - 1)
        flush(("ag", a))

    def tiny_send(a):
        for step in range(1, chips):
            block = r.tiny.at[a, chip]
            peer = lax.rem(chip + step, chips)
            send(block, block, r.tiny_s.at[a], r.tiny_r.at[a], (2 * peer + core, mine))
        later("end", r.tiny.at[a, pl.ds(0, chips - 1)], r.tiny_s.at[a])

    def tiny_wait(a):
        settle(r.tiny.at[a, pl.ds(0, chips - 1)], r.tiny_r.at[a])

    group = min(chips, 4)
    first_tap = lax.div(2 * deep * chip, INNER)
    margin = 2 * deep * chip - first_tap * INNER

    def deep_make(u):
        flush("deep")
        field_of, back_of = (0, 3) if u == DEF else (1, 2)
        for g in range(chips // group):
            fields = dma(
                far_blocks.at[field_of, pl.ds(g * group, group)], r.taken, r.take_sem.at[2]
            )
            fields.start()

            def fetch(m):
                return dma(
                    far_blocks.at[back_of, g * group + m], r.drawn.at[m % 2], r.take_sem.at[m % 2]
                )

            for m in range(min(2, group)):
                fetch(m).start()
            for m in range(group):
                fetch(m).wait()

                def lower(i, carry):
                    rows = pl.ds(pl.multiple_of(m * ROWS + i * 32, 32), 32)
                    there = pl.ds(pl.multiple_of(i * 32, 32), 32)
                    r.yall[rows, :] = r.drawn[m % 2, there, :].astype(BF)
                    return carry

                lax.fori_loop(0, ROWS // 32, lower, 0)
                if m + 2 < group:
                    fetch(m + 2).start()
            fields.wait()

            def one(kk, carry):
                k = jnp.minimum(first_tap + kk, TAPS - 1)
                down, across = steps_of(k)

                def image(i, share):
                    m, s = lax.div(i, SLOTS), lax.rem(i, SLOTS)
                    rows = pl.ds(pl.multiple_of(i * PIXELS, PIXELS), PIXELS)
                    there = pl.ds(pl.multiple_of(s * PIXELS, PIXELS), PIXELS)
                    field = r.taken[m, there, :].astype(BF)
                    tiny = r.tiny.at[0, g * group + m, s]
                    flat = tiny[18:19, :] == 0.0
                    dr = jnp.where(flat, r.geo[0, 0], r.geo[1, 0])
                    dc = jnp.where(flat, r.geo[0, 1], r.geo[1, 1])
                    hit = jnp.where((dr == down) & (dc == across), 1.0, 0.0).astype(BF)
                    if u == CON:
                        r.xall[rows, :] = mm(hit, field, NN).astype(BF)
                        return share
                    fy, fx = tiny[pl.ds(2 * k, 1), :], tiny[pl.ds(2 * k + 1, 1), :]
                    ay = jnp.where(dr == -down, 1.0 - fy, jnp.where(dr == -down - 1, fy, 0.0))
                    ax = jnp.where(
                        dc == -across, 1.0 - fx, jnp.where(dc == -across - 1, fx, 0.0)
                    )
                    r.xall[rows, :] = mm((ay * ax).astype(BF), field, TN).astype(BF)
                    shift = r.tiny[1, g * group + m, s].astype(BF)
                    moved = mm(shift, hit, NN).astype(BF)
                    return share + mm(moved, field, NN)

                at = pl.ds(pl.multiple_of(kk * INNER, INNER), INNER)
                zero = jnp.zeros((24, INNER) if u == DEF else (8, 128), F32)
                share = lax.fori_loop(0, group * SLOTS, image, zero)
                part = mm(r.xall[...], r.yall[...], TN)
                if g == 0:
                    grad[at, :] = part
                else:
                    grad[at, :] += part
                if u == DEF:
                    if g == 0:
                        r.goff[:, at] = share
                    else:
                        r.goff[:, at] += share
                return carry

            lax.fori_loop(0, taps, one, 0)
        away = pl.ds(pl.multiple_of(margin + (1 - core) * deep, 8), deep)
        send(grad.at[away], r.cored, r.core_s.at[u], r.core_r.at[u], sibling)
        later("deep", r.cored, r.core_s.at[u])
        if u == DEF:
            send(r.goff, r.coreo, r.core_s.at[OFF], r.core_r.at[OFF], sibling)

    def deep_core(u):
        settle(r.cored, r.core_r.at[u])
        half = deep // 2
        step = math.gcd(half, 32)
        for q in range(2):
            target = r.b3.at[(2 if u == DEF else 0) + q]

            def body(i, carry):
                at = pl.multiple_of(i * step, 8)
                here = grad[pl.ds(pl.multiple_of(margin + core * deep + q * half + at, 8), step), :]
                target[pl.ds(at, step), :] = here + r.cored[pl.ds(q * half + at, step), :]
                return carry

            lax.fori_loop(0, half // step, body, 0)
        if u == DEF:
            settle(r.goff, r.core_s.at[OFF])
            settle(r.coreo, r.core_r.at[OFF])
            accumulate(r.goff, r.coreo)
            z1(OFF)
        z1(u)

    images, between, acc, up = r.images, r.between, r.acc, r.up
    ig = [r.ig[i : i + 1, :] for i in range(4)]
    ib = [r.ib[i : i + 1, :] for i in range(4)]
    bg = [r.bg[i : i + 1, :] for i in range(2)]
    bb = [r.bb[i : i + 1, :] for i in range(2)]

    def geometry():
        q = lax.broadcasted_iota(jnp.int32, (PIXELS, PIXELS), 1)
        p = lax.broadcasted_iota(jnp.int32, (PIXELS, PIXELS), 0)

        def place_of(at, kind):
            if kind:
                row = lax.shift_right_logical(at, 2)
                return row, at - row * SHORT
            row = (at >= LONG).astype(jnp.int32) + (at >= 2 * LONG).astype(jnp.int32)
            row = row + (at >= 3 * LONG).astype(jnp.int32)
            return row, at - row * LONG

        for kind in range(2):
            row_q, col_q = place_of(q, kind)
            row_p, col_p = place_of(p, kind)
            r.geo[kind, 0] = row_q - row_p
            r.geo[kind, 1] = col_q - col_p

            def hot(k, carry):
                down, across = steps_of(k)
                hit = (r.geo[kind, 0] == down) & (r.geo[kind, 1] == across)
                r.tmat[kind, k] = jnp.where(hit, 1.0, 0.0).astype(BF)
                return carry

            lax.fori_loop(0, TAPS, hot, 0)

    def shifted(s, k):
        return r.tmat[orient[s], k]

    loads.images_h.wait()
    loads.red_h.wait()
    r.a1[...] = mm(images[...], r.redwid[...], NN)
    loads.wid_h = load(7, r.wid_h, r.redwid)
    pl.semaphore_wait(barrier, everyone - 1)
    narrow_stats(r.a1, 0, geometry)
    norm_silu(r.a1, 0, ig[0], ib[0], r.inner, True)
    gather_start(0)

    loads.off_h.wait()
    inner = r.inner
    lane = lax.broadcasted_iota(jnp.int32, (PIXELS, OFFSETS), 1)
    for s in range(SLOTS):

        def gather(k, carry):
            col = mm(shifted(s, k), inner[slot_rows(s), :], NN).astype(BF)
            return carry + mm(col, tap(r.off, k), NN)

        offsets = lax.fori_loop(0, TAPS, gather, jnp.zeros((PIXELS, OFFSETS), F32))
        frac = sigmoid(offsets)
        r.frac[slot_rows(s), :] = frac
        coarse = frac.astype(BF)
        fine = (frac - coarse.astype(F32)).astype(BF)
        unit = r.tmat[0, TAPS // 2]
        put = r.tiny.at[0, chip, s]
        put[...] = jnp.zeros((24, PIXELS), F32) + orient[s].astype(F32)
        put[0:OFFSETS, :] = mm(coarse, unit, TN) + mm(fine, unit, TN)
    tiny_send(0)

    def bilinear(s, k):
        down, across = steps_of(k)
        frac = r.frac[slot_rows(s), :]
        fy = jnp.sum(jnp.where(lane == 2 * k, frac, 0.0), axis=1, keepdims=True)
        fx = jnp.sum(jnp.where(lane == 2 * k + 1, frac, 0.0), axis=1, keepdims=True)
        dr, dc = r.geo[orient[s], 0], r.geo[orient[s], 1]
        in_y = (dr == down, dr == down + 1)
        in_x = (dc == across, dc == across + 1)
        ay = jnp.where(in_y[0], 1.0 - fy, jnp.where(in_y[1], fy, 0.0))
        ax = jnp.where(in_x[0], 1.0 - fx, jnp.where(in_x[1], fx, 0.0))
        return fy, fx, ay, ax, in_y, in_x

    loads.def_h.wait()
    acc[...] = jnp.zeros((ROWS, INNER), F32)

    def sample(k, carry):
        for s in range(SLOTS):
            _, _, ay, ax, _, _ = bilinear(s, k)
            weight = (ay * ax).astype(BF)
            r.wmat[s, k] = weight
            r.turned[slot_rows(s), :] = mm(weight, inner[slot_rows(s), :], NN).astype(BF)
        acc[...] += mm(r.turned[...], tap(r.dfmcon, k), NN)
        return carry

    lax.fori_loop(0, TAPS, sample, 0)
    loads.con_h = load(8, r.con_h, r.dfmcon)
    r.a2[...] = acc[...]
    narrow_stats(r.a2, 1, lambda: gather_step(0, 1))
    norm_silu(r.a2, 1, ig[1], ib[1], r.hidden, False)

    def widen(source, weight, target):
        def step(n, carry):
            rows = pl.ds(pl.multiple_of(n * 512, 512), 512)
            target[n] = mm(source[...], weight[rows, :], NT)
            return carry

        lax.fori_loop(0, CHANNELS // 512, step, 0)

    loads.exp_h.wait()
    widen(r.hidden, r.exp, r.a3)
    wide_stats(r.a3, 0)
    for n, cs in enumerate(blocks):
        mean = r.stw[0, 0:1, cs]
        steep = r.stw[0, 1:2, cs] * bg[0][:, 512 * n : 512 * n + 512]
        bias = bb[0][:, 512 * n : 512 * n + 512]

        def join(rs, lv, carry):
            z = (r.a3[n, rs, :] - mean) * steep + bias + images[rs, cs].astype(F32)
            between[rs, cs] = (z * sigmoid(z)).astype(BF)
            return carry

        sweep(join, 0)

    loads.nar_h.wait()
    r.b1[...] = mm(between[...], r.nar[...], NN)

    def work_b1():
        gather_end(0)
        tiny_wait(0)

    narrow_stats(r.b1, 2, work_b1)
    norm_silu(r.b1, 2, ig[2], ib[2], r.narrow, True)
    gather_start(1)

    loads.con_h.wait()
    acc[...] = jnp.zeros((ROWS, INNER), F32)

    def convolve(k, carry):
        for s in range(SLOTS):
            r.turned[slot_rows(s), :] = mm(
                shifted(s, k), r.narrow[slot_rows(s), :], NN
            ).astype(BF)
        acc[...] += mm(r.turned[...], tap(r.dfmcon, k), NN)
        return carry

    lax.fori_loop(0, TAPS, convolve, 0)
    r.b2[...] = acc[...]
    narrow_stats(r.b2, 3, lambda: gather_step(1, 1))
    norm_silu(r.b2, 3, ig[3], ib[3], r.mixed, False)

    loads.wid_h.wait()
    widen(r.mixed, r.redwid, r.b3)
    wide_stats(r.b3, 1)

    loads.cot_h.wait()

    def last(n, rs, cs, lv, pre):
        z = pre + between[rs, cs].astype(F32)
        sg = sigmoid(z)
        r.obuf[rs, cs] = (lv * (z * sg)).astype(BF)
        return r.dwide[rs, cs].astype(F32) * (lv * (sg * (1.0 + z * (1.0 - sg))))

    wide_cotangent(
        2, r.b3, 1, bg[1], bb[1], last, nothing, lambda: gather_end(1)
    )
    out_copy = dma(r.obuf, r.out_h, r.out_sem.at[0])
    out_copy.start()
    wide_begin(WID, r.dwide, r.mixed)
    acc[...] = mm(r.dwide[...], r.redwid[...], NN)
    loads.red_h = load(9, r.red_h, r.redwid)
    wide_core(WID)
    narrow_cotangent(r.b2, 3, ig[3], ib[3], 4, True)
    gather_start(2)

    acc[...] = jnp.zeros((ROWS, INNER), F32)

    def spread(k, carry):
        for s in range(SLOTS):
            r.turned[slot_rows(s), :] = mm(
                shifted(s, TAPS - 1 - k), r.dn[slot_rows(s), :], NN
            ).astype(BF)
        acc[...] += mm(r.turned[...], tap(r.dfmcon, k), NT)
        return carry

    lax.fori_loop(0, TAPS, spread, 0)
    loads.def_h = load(10, r.def_h, r.dfmcon)
    wide_step(WID, 1)
    narrow_cotangent(r.b1, 2, ig[2], ib[2], 5, False, lambda: gather_step(2, 1))
    wide_begin(NAR, between, r.dn)

    def add_back(n, carry):
        rows = pl.ds(pl.multiple_of(n * 512, 512), 512)
        up[n] += mm(r.dn[...], r.nar[rows, :], NT)
        return carry

    lax.fori_loop(0, CHANNELS // 512, add_back, 0)
    wide_step(WID, 2)
    wide_core(NAR)

    def first(n, rs, cs, lv, pre):
        z = pre + images[rs, cs].astype(F32)
        sg = sigmoid(z)
        return up[n, rs, :] * (sg * (1.0 + z * (1.0 - sg)))

    wide_cotangent(3, r.a3, 0, bg[0], bb[0], first, nothing, nothing)
    wide_begin(EXP, r.dwide, r.hidden)
    acc[...] = mm(r.dwide[...], r.exp[...], NN)
    wide_step(NAR, 1)
    wide_core(EXP)
    z2(WID)

    def work_b():
        gather_end(2)
        deep_make(CON)

    narrow_cotangent(r.a2, 1, ig[1], ib[1], 6, True, work_b)
    gather_start(3)
    deep_core(CON)
    wide_step(NAR, 2)
    z3(WID)

    loads.def_h.wait()
    acc[...] = jnp.zeros((ROWS, INNER), F32)
    r.doff[...] = jnp.zeros((ROWS, OFFSETS), F32)

    def unsample(k, carry):
        r.turned[...] = mm(r.dn[...], tap(r.dfmcon, k), NT).astype(BF)
        for s in range(SLOTS):
            rs = slot_rows(s)
            back = r.turned[rs, :]
            pairs = mm(back, inner[rs, :], NT)
            fy, fx, ay, ax, in_y, in_x = bilinear(s, k)
            slope_y = jnp.where(in_y[1], ax, 0.0) - jnp.where(in_y[0], ax, 0.0)
            slope_x = jnp.where(in_x[1], ay, 0.0) - jnp.where(in_x[0], ay, 0.0)
            to_y = jnp.sum(pairs * slope_y, axis=1, keepdims=True) * (fy * (1.0 - fy))
            to_x = jnp.sum(pairs * slope_x, axis=1, keepdims=True) * (fx * (1.0 - fx))
            r.doff[rs, :] += jnp.where(lane == 2 * k, to_y, 0.0) + jnp.where(
                lane == 2 * k + 1, to_x, 0.0
            )
            acc[rs, :] += mm(r.wmat[s, k], back, TN)
        return carry

    lax.fori_loop(0, TAPS, unsample, 0)
    for s in range(SLOTS):
        put = r.tiny.at[1, chip, s]
        put[...] = jnp.zeros((24, PIXELS), F32)
        put[0:OFFSETS, :] = mm(
            r.doff[slot_rows(s), :].astype(BF), r.tmat[0, TAPS // 2], TN
        )
    tiny_send(1)
    gather_step(3, 1)

    def untap(k, carry):
        for s in range(SLOTS):
            rs = slot_rows(s)
            moved = mm(shifted(s, TAPS - 1 - k), r.doff[rs, :].astype(BF), NN).astype(BF)
            acc[rs, :] += mm(moved, tap(r.off, k), NT)
        return carry

    lax.fori_loop(0, TAPS, untap, 0)
    z4(WID)
    wide_step(EXP, 1)
    z2(CON)
    z_clear(WID)
    narrow_cotangent(r.a1, 0, ig[0], ib[0], 7, False, lambda: z2(NAR))
    wide_begin(RED, images, r.dn)

    out_copy.wait()
    loads.red_h.wait()

    def finish(n, carry):
        rows = pl.ds(pl.multiple_of(n * 512, 512), 512)
        r.obuf[:, rows] = (up[n] + mm(r.dn[...], r.redwid[rows, :], NT)).astype(BF)
        return carry

    lax.fori_loop(0, CHANNELS // 512, finish, 0)
    grad_copy = dma(r.obuf, r.grad_h, r.out_sem.at[1])
    grad_copy.start()
    wide_step(EXP, 2)
    wide_core(RED)
    z3(CON)
    z3(NAR)
    gather_end(3)
    tiny_wait(1)
    z4(CON)
    z_clear(CON)
    deep_make(DEF)
    wide_step(RED, 1)
    z2(EXP)
    deep_core(DEF)
    z4(NAR)
    z_clear(NAR)
    wide_step(RED, 2)
    z3(EXP)
    z4(EXP)
    z2(OFF)
    z2(DEF)
    z2(RED)
    z3(OFF)
    z3(DEF)
    z3(RED)
    z4(OFF)
    z4(DEF)
    z4(RED)
    for u in (EXP, OFF, DEF, RED):
        z_clear(u)
    grad_copy.wait()
    for tag in list(waiting):
        flush(tag)


def per_device(
    images,
    counts,
    orientation,
    cotangent,
    reducer,
    offseter,
    deformer,
    expander,
    narrower,
    convolver,
    widener,
    inner_gains,
    inner_biases,
    broad_gains,
    broad_biases,
):
    dp, outer = lax.axis_size("dp"), lax.axis_size("outer")
    chips, bits, wide, deep, taps = layout(dp)
    buffers = scratch(dp, outer)
    smem = pl.BlockSpec(memory_space=pltpu.SMEM)
    vmem = pl.BlockSpec(memory_space=pltpu.VMEM)
    far = pl.BlockSpec(memory_space=pl.ANY)
    shape = jax.ShapeDtypeStruct
    inputs = dict(
        counts=(smem, counts),
        orient=(smem, orientation),
        ig=(vmem, inner_gains),
        ib=(vmem, inner_biases),
        bg=(vmem, broad_gains),
        bb=(vmem, broad_biases),
        images_h=(far, images.reshape(ROWS, CHANNELS)),
        cot_h=(far, cotangent.reshape(ROWS, CHANNELS)),
        red_h=(far, reducer),
        off_h=(far, offseter),
        def_h=(far, deformer),
        exp_h=(far, expander),
        nar_h=(far, narrower),
        con_h=(far, convolver),
        wid_h=(far, widener),
    )
    outputs = dict(
        out_h=(far, shape((ROWS, CHANNELS), BF)),
        grad_h=(far, shape((ROWS, CHANNELS), BF)),
        g_red=(far, shape((wide, INNER), F32)),
        g_off=(far, shape((24, taps * INNER), F32)),
        g_def=(far, shape((deep, INNER), F32)),
        g_exp=(far, shape((wide, INNER), F32)),
        g_nar=(far, shape((wide, INNER), F32)),
        g_con=(far, shape((deep, INNER), F32)),
        g_wid=(far, shape((wide, INNER), F32)),
        g_ig=(vmem, shape((4, INNER), F32)),
        g_ib=(vmem, shape((4, INNER), F32)),
        g_bg=(vmem, shape((2, CHANNELS), F32)),
        g_bb=(vmem, shape((2, CHANNELS), F32)),
        far_blocks=(far, shape((4, chips, ROWS, INNER), F32)),
    )
    names = list(inputs) + list(outputs) + list(buffers)
    outs = pl.pallas_call(
        functools.partial(kernel, dp, outer, names),
        out_shape=[spec for _, spec in outputs.values()],
        in_specs=[space for space, _ in inputs.values()],
        out_specs=[space for space, _ in outputs.values()],
        scratch_shapes=list(buffers.values()),
        compiler_params=pltpu.CompilerParams(
            collective_id=0, has_side_effects=True, vmem_limit_bytes=62 * 1024 * 1024
        ),
        name="chain",
    )(*[value for _, value in inputs.values()])
    out, grad, g_red, g_off, g_def, g_exp, g_nar, g_con, g_wid, g_ig, g_ib, g_bg, g_bb, _ = outs
    place = lax.axis_index("dp")
    inner_share, broad_share = INNER // dp, CHANNELS // dp
    begin = 2 * deep * (place // 2) % INNER + deep * (place % 2)
    g_off = lax.dynamic_slice_in_dim(g_off.T, begin, deep, 0)[:, :OFFSETS]
    return (
        out.reshape(SLOTS, PIXELS, CHANNELS),
        grad.reshape(SLOTS, PIXELS, CHANNELS),
        g_red,
        g_off,
        g_def,
        g_exp,
        g_nar,
        g_con,
        g_wid,
        lax.dynamic_slice_in_dim(g_ig, place * inner_share, inner_share, 1),
        lax.dynamic_slice_in_dim(g_ib, place * inner_share, inner_share, 1),
        lax.dynamic_slice_in_dim(g_bg, place * broad_share, broad_share, 1),
        lax.dynamic_slice_in_dim(g_bb, place * broad_share, broad_share, 1),
    )


def solution(mesh):
    spread = P(("dp", "outer"), None, None)
    in_specs = (spread, P(), P(("dp", "outer")), spread) + (P(),) * 11
    out_specs = (spread, spread) + (P("dp", None),) * 7 + (P(None, "dp"),) * 4
    return jax.shard_map(
        per_device, mesh=mesh, in_specs=in_specs, out_specs=out_specs, check_vma=False
    )
```

time: 783 us -> 383 us (0.49)
  waiting for transfers between devices: 562 us -> 0 us
  Pallas kernels: 168 us -> 365 us
  blocking collectives: 21.7 us -> 0 us
  between operations: 14.2 us -> 0.71 us
    reduce_scatter x6 -> x0, waiting for transfers between devices: 370 us -> none  [per_device(): lax.psum_scatter(part, 'dp', scatter_dimension=0, tiled=True)]
    pallas_call x1, Pallas kernels: 168 us -> 365 us  [per_device(): pl.pallas_call(functools.partial(kernel, dp, outer, names), out_shape=[sp...]
    psum x1 -> x0, waiting for transfers between devices: 146 us -> none  [per_device(): parts = lax.psum(parts, 'outer')]
    unnamed x9 -> x0, waiting for transfers between devices: 46.1 us -> none
    psum x1 -> x0, blocking collectives: 21.7 us -> none  [per_device(): parts = lax.psum(parts, 'outer')]
  transfers between devices with their start and end apart: 8 -> 0, of which waited for: 8 -> 0; matrix products, arithmetic and copies ran while one was open for 1% -> 0% of each run, Pallas kernels for 0% -> 0%
where the time goes in v2:
time: 383 us; the launch traced here: 382 us
  Pallas kernels  365 us (95%)
  local copies, waits for them, and re-layouts  16.4 us (4%)
    pallas_call x1, Pallas kernels, per_device(): pl.pallas_call(functools.partial(kernel, dp, outer, names), out_shape=[sp...  365 us
    unnamed x23, local copies, waits for them, and re-layouts  12.2 us

profile of v2, /device:TPU:0, one launch (start us, length us, event | category | flops | bytes accessed | tf_op | source)
XLA Modules:
  0.0 382.1 jit_solution(13287710793608593946)
XLA Ops:
  0.6 2.4 copy.28.refs_9_
  3.0 364.9 %chain.1 = (bf16[288,2048]{1,0:T(8,128)(2,1)}, bf16[288,2048]{1,0:T(8,128)(2,1)}, f32[256,512]{1,0:T(8,128)}, f32[24,1536]{1,0:T(8,128)}, f32[576,512]{1,0:T(8,1...) custom-call(s32[32]{0:T(128)} %refs_0_.1, ...), custom_call_target="tpu_custom_call" | custom-call | tf_op jit(solution)/shard_map/chain/pallas_call | solution.py:1128
  368.0 1.6 dynamic-slice_bitcast_fusion
  369.6 1.3 constant_dynamic-slice_fusion.2
  371.0 1.3 constant_dynamic-slice_fusion
  372.2 0.0 copy-start.2
  372.2 2.5 copy.37
  374.7 0.0 copy-done.2
  374.7 0.0 copy-start.6
  374.7 0.0 copy-start.1
  374.7 1.0 copy.38
  375.8 0.4 copy-done.6
  376.1 0.8 copy.39
  376.9 0.0 copy-done.1
  376.9 0.0 copy-start.5
  376.9 1.0 copy.40
  377.9 0.4 copy-done.5
  378.3 0.8 copy.41
  379.1 0.0 copy-done.4
  379.1 0.8 copy.42
  379.9 0.0 copy-done
  379.9 1.0 copy.43
  380.9 0.4 copy-done.3
  381.3 0.8 copy.44
  (3 shorter events, 0.0 us)
Async XLA Ops:
  372.2 2.5 copy-start.2
  374.7 1.4 copy-start.6
  374.7 2.2 copy-start.1
  376.9 1.4 copy-start.5
  376.9 2.2 copy-start.4
  378.3 1.6 copy-start
  379.9 1.4 copy-start.3

commit v3 on v2

--- a/solution.py
+++ b/solution.py
@@ -69,7 +69,7 @@
         exp=vmem((CHANNELS, INNER), BF),
         nar=vmem((CHANNELS, INNER), BF),
         dfmcon=vmem((TAPS * INNER, INNER), BF),
-        off=vmem((TAPS * INNER, OFFSETS), BF),
+        off=vmem((OFFSETS, TAPS * INNER), BF),
         a1=vmem((ROWS, INNER), F32),
         a2=vmem((ROWS, INNER), F32),
         b1=vmem((ROWS, INNER), F32),
@@ -97,7 +97,7 @@
         pool=vmem((3, chips, wide, INNER), F32),
         corel=vmem((chips, wide, INNER), F32),
         land=vmem((2, 2, chips - 1, wide, INNER // 2), F32),
-        zwide=vmem((2, 3, wide, INNER), F32),
+        zwide=vmem((3, 3, wide, INNER), F32),
         tiny=vmem((2, chips, SLOTS, 24, PIXELS), F32),
         give=vmem((ROWS, INNER), F32),
         taken=vmem((group, ROWS, INNER), F32),
@@ -111,9 +111,10 @@
         coreo=vmem((24, taps * INNER), F32),
         zoff=vmem((2, 24, taps * INNER), F32),
         free=pltpu.SemaphoreType.REGULAR,
+        credit=pltpu.SemaphoreType.REGULAR((2, bits)),
         load_sem=dma((11,)),
         out_sem=dma((2,)),
-        res_sem=dma((7, 2)),
+        res_sem=dma((7, 4)),
         xn_s=dma((8,)),
         xn_r=dma((8,)),
         xw_s=dma((4, 2)),
@@ -128,8 +129,8 @@
         ag_r=dma((4, 2, bits)),
         tiny_s=dma((2,)),
         tiny_r=dma((2,)),
-        z_s=dma((7, 2, 3)),
-        z_r=dma((7, 2, 3)),
+        z_s=dma((7, 4, 3)),
+        z_r=dma((7, 4, 3)),
     )
 
 
@@ -440,6 +441,9 @@
     def tap(ref, k):
         return ref[pl.ds(pl.multiple_of(k * INNER, INNER), INNER), :]
 
+    def offset_tap(k):
+        return r.off[:, pl.ds(pl.multiple_of(k * INNER, INNER), INNER)]
+
     def slot_rows(s):
         return pl.ds(s * PIXELS, PIXELS)
 
@@ -459,32 +463,38 @@
     }
     pool, land, grad, far_blocks = r.pool, r.land, r.grad, r.far_blocks
 
+    deep_parts = 4 if deep % 32 == 0 else 2
+
     def z_parts(u):
         if u in nth:
             if u == RED:
                 hold = [r.a3.at[i, pl.ds(0, wide)] for i in range(3)]
             else:
-                hold = [r.zwide.at[nth[u] % 2, i] for i in range(3)]
+                hold = [r.zwide.at[nth[u], i] for i in range(3)]
             for hs in halves:
                 yield tuple(ref.at[:, hs] for ref in hold) + (result[u].at[:, hs],)
         elif u == OFF:
             yield r.goff, r.zoff.at[0], r.zoff.at[1], result[u]
         else:
-            for q in range(2):
-                source = r.b3.at[(2 if u == DEF else 0) + q]
+            for q in range(deep_parts):
+                back, at = divmod(q, deep_parts // 2)
+                source = r.b3.at[(2 if u == DEF else 0) + back]
                 if u == DEF:
-                    first, second = (r.b1, r.a2) if q == 0 else (r.b2, r.a3.at[3])
+                    first, second = (r.b1, r.a2) if back == 0 else (r.b2, r.a3.at[3])
                 else:
-                    first, second = r.zdeep.at[0, q], r.zdeep.at[1, q]
-                rows = pl.ds(0, deep // 2)
-                out = result[u].at[pl.ds(q * (deep // 2), deep // 2)]
+                    first, second = r.zdeep.at[0, back], r.zdeep.at[1, back]
+                size = deep // deep_parts
+                rows = pl.ds(at * size, size)
+                out = result[u].at[pl.ds(q * size, size)]
                 yield source.at[rows], first.at[rows], second.at[rows], out
 
     def z_sems(u, q, step):
         return r.z_s.at[u, q, step], r.z_r.at[u, q, step]
 
-    def z1(u):
+    def z1(u, some=None):
         for q, (source, first, second, out) in enumerate(z_parts(u)):
+            if some is not None and q not in some:
+                continue
             sent, received = z_sems(u, q, 0)
 
             @pl.when(outside)
@@ -493,8 +503,10 @@
 
             later(("z", u), source, sent, outside)
 
-    def z2(u):
+    def z2(u, some=None):
         for q, (source, first, second, out) in enumerate(z_parts(u)):
+            if some is not None and q not in some:
+                continue
             sent, received = z_sems(u, q, 1)
 
             @pl.when(inside)
@@ -505,8 +517,10 @@
 
             later(("z", u), source, sent, inside)
 
-    def z3(u):
+    def z3(u, some=None):
         for q, (source, first, second, out) in enumerate(z_parts(u)):
+            if some is not None and q not in some:
+                continue
             sent, received = z_sems(u, q, 2)
 
             @pl.when(inside)
@@ -518,8 +532,10 @@
 
             later(("zl", u), second, sent, inside)
 
-    def z4(u):
+    def z4(u, some=None):
         for q, (source, first, second, out) in enumerate(z_parts(u)):
+            if some is not None and q not in some:
+                continue
 
             @pl.when(outside)
             def _():
@@ -573,6 +589,8 @@
         for h in range(2):
             p, first, count, (sent, received), region = step_place(u, h, t)
             toward = flip(chip, orders[h][t])
+            if u == RED:
+                pl.semaphore_wait(r.credit.at[h, t], 1)
             for j in range(count):
                 send(
                     pool.at[p, piece(h, t, j, toward), :, halves[h]],
@@ -589,10 +607,17 @@
             settle(region, received)
             if t == bits - 1:
                 mix(list(z_parts(u))[h][0], pool.at[p, chip, :, halves[h]], land.at[p, h, first])
-                continue
-            for j in range(count):
-                accumulate(
-                    pool.at[p, piece(h, t, j, chip), :, halves[h]], land.at[p, h, first + j]
+            else:
+                for j in range(count):
+                    accumulate(
+                        pool.at[p, piece(h, t, j, chip), :, halves[h]], land.at[p, h, first + j]
+                    )
+            if u == NAR:
+                pl.semaphore_signal(
+                    r.credit.at[h, t],
+                    inc=1,
+                    device_id=(2 * flip(chip, orders[h][t]) + core, mine),
+                    device_id_type=MESH,
                 )
 
     def wide_core(u):
@@ -604,7 +629,6 @@
             return carry
 
         lax.fori_loop(0, chips, step, 0)
-        wide_send(u, 0)
 
     def wide_step(u, t):
         wide_add(u, t - 1)
@@ -620,15 +644,16 @@
                 value = flip(value, orders[h][i])
         return value
 
-    def gather_send(a, t):
+    def gather_send(a, t, some=None):
         for h in range(2):
             partner = flip(chip, orders[h][t])
             sent, received = r.ag_s.at[a, h, t], r.ag_r.at[a, h, t]
-            for j in range(1 << t):
+            for j in range(1 << t) if some is None else some:
                 block = far_blocks.at[a, held_at(h, j), :, halves[h]]
                 source = r.give.at[:, halves[h]] if j == 0 else block
                 send(source, block, sent, received, (2 * partner + core, mine))
-            later(("ag", a), far_blocks.at[a, pl.ds(0, 1 << t), :, halves[h]], sent)
+            if some is None or 0 in some:
+                later(("ag", a), far_blocks.at[a, pl.ds(0, 1 << t), :, halves[h]], sent)
 
     def gather_start(a):
         block = far_blocks.at[a, chip]
@@ -640,9 +665,18 @@
         for h in range(2):
             settle(far_blocks.at[a, pl.ds(0, 1 << t), :, halves[h]], r.ag_r.at[a, h, t])
 
-    def gather_step(a, t):
+    def gather_step(a, t, some=None):
         gather_wait(a, t - 1)
-        gather_send(a, t)
+        gather_send(a, t, some)
+
+    def gather_first(a, t):
+        if t < bits:
+            gather_send(a, t, [0])
+
+    def gather_rest(a):
+        for t in range(1, bits):
+            gather_wait(a, t - 1)
+            gather_send(a, t, range(1 if t == 1 else 0, 1 << t))
 
     def gather_end(a):
         gather_wait(a, bits - 1)
@@ -759,8 +793,6 @@
             settle(r.goff, r.core_s.at[OFF])
             settle(r.coreo, r.core_r.at[OFF])
             accumulate(r.goff, r.coreo)
-            z1(OFF)
-        z1(u)
 
     images, between, acc, up = r.images, r.between, r.acc, r.up
     ig = [r.ig[i : i + 1, :] for i in range(4)]
@@ -813,7 +845,7 @@
 
         def gather(k, carry):
             col = mm(shifted(s, k), inner[slot_rows(s), :], NN).astype(BF)
-            return carry + mm(col, tap(r.off, k), NN)
+            return carry + mm(col, offset_tap(k), NT)
 
         offsets = lax.fori_loop(0, TAPS, gather, jnp.zeros((PIXELS, OFFSETS), F32))
         frac = sigmoid(offsets)
@@ -853,7 +885,7 @@
     lax.fori_loop(0, TAPS, sample, 0)
     loads.con_h = load(8, r.con_h, r.dfmcon)
     r.a2[...] = acc[...]
-    narrow_stats(r.a2, 1, lambda: gather_step(0, 1))
+    narrow_stats(r.a2, 1, lambda: gather_first(0, 1))
     norm_silu(r.a2, 1, ig[1], ib[1], r.hidden, False)
 
     def widen(source, weight, target):
@@ -866,7 +898,7 @@
 
     loads.exp_h.wait()
     widen(r.hidden, r.exp, r.a3)
-    wide_stats(r.a3, 0)
+    wide_stats(r.a3, 0, lambda: gather_rest(0))
     for n, cs in enumerate(blocks):
         mean = r.stw[0, 0:1, cs]
         steep = r.stw[0, 1:2, cs] * bg[0][:, 512 * n : 512 * n + 512]
@@ -903,12 +935,12 @@
 
     lax.fori_loop(0, TAPS, convolve, 0)
     r.b2[...] = acc[...]
-    narrow_stats(r.b2, 3, lambda: gather_step(1, 1))
+    narrow_stats(r.b2, 3, lambda: gather_first(1, 1))
     norm_silu(r.b2, 3, ig[3], ib[3], r.mixed, False)
 
     loads.wid_h.wait()
     widen(r.mixed, r.redwid, r.b3)
-    wide_stats(r.b3, 1)
+    wide_stats(r.b3, 1, lambda: gather_rest(1))
 
     loads.cot_h.wait()
 
@@ -927,8 +959,7 @@
     acc[...] = mm(r.dwide[...], r.redwid[...], NN)
     loads.red_h = load(9, r.red_h, r.redwid)
     wide_core(WID)
-    narrow_cotangent(r.b2, 3, ig[3], ib[3], 4, True)
-    gather_start(2)
+    narrow_cotangent(r.b2, 3, ig[3], ib[3], 4, True, lambda: wide_send(WID, 0))
 
     acc[...] = jnp.zeros((ROWS, INNER), F32)
 
@@ -942,8 +973,12 @@
 
     lax.fori_loop(0, TAPS, spread, 0)
     loads.def_h = load(10, r.def_h, r.dfmcon)
-    wide_step(WID, 1)
-    narrow_cotangent(r.b1, 2, ig[2], ib[2], 5, False, lambda: gather_step(2, 1))
+
+    def work_d():
+        gather_start(2)
+        wide_step(WID, 1)
+
+    narrow_cotangent(r.b1, 2, ig[2], ib[2], 5, False, work_d)
     wide_begin(NAR, between, r.dn)
 
     def add_back(n, carry):
@@ -952,7 +987,6 @@
         return carry
 
     lax.fori_loop(0, CHANNELS // 512, add_back, 0)
-    wide_step(WID, 2)
     wide_core(NAR)
 
     def first(n, rs, cs, lv, pre):
@@ -960,22 +994,30 @@
         sg = sigmoid(z)
         return up[n, rs, :] * (sg * (1.0 + z * (1.0 - sg)))
 
-    wide_cotangent(3, r.a3, 0, bg[0], bb[0], first, nothing, nothing)
+    def work_c():
+        for t in range(1, bits):
+            gather_step(2, t)
+
+    def work_more_c():
+        for t in range(2, bits + 1):
+            wide_step(WID, t)
+
+    wide_cotangent(3, r.a3, 0, bg[0], bb[0], first, work_c, work_more_c)
     wide_begin(EXP, r.dwide, r.hidden)
     acc[...] = mm(r.dwide[...], r.exp[...], NN)
-    wide_step(NAR, 1)
     wide_core(EXP)
-    z2(WID)
 
     def work_b():
+        wide_send(NAR, 0)
+        z2(WID)
         gather_end(2)
         deep_make(CON)
 
     narrow_cotangent(r.a2, 1, ig[1], ib[1], 6, True, work_b)
     gather_start(3)
     deep_core(CON)
-    wide_step(NAR, 2)
-    z3(WID)
+    early, late = range(deep_parts // 2), range(deep_parts // 2, deep_parts)
+    z1(CON, early)
 
     loads.def_h.wait()
     acc[...] = jnp.zeros((ROWS, INNER), F32)
@@ -1006,21 +1048,28 @@
             r.doff[slot_rows(s), :].astype(BF), r.tmat[0, TAPS // 2], TN
         )
     tiny_send(1)
-    gather_step(3, 1)
 
     def untap(k, carry):
         for s in range(SLOTS):
             rs = slot_rows(s)
             moved = mm(shifted(s, TAPS - 1 - k), r.doff[rs, :].astype(BF), NN).astype(BF)
-            acc[rs, :] += mm(moved, tap(r.off, k), NT)
+            acc[rs, :] += mm(moved, offset_tap(k), NN)
         return carry
 
     lax.fori_loop(0, TAPS, untap, 0)
-    z4(WID)
-    wide_step(EXP, 1)
-    z2(CON)
-    z_clear(WID)
-    narrow_cotangent(r.a1, 0, ig[0], ib[0], 7, False, lambda: z2(NAR))
+
+    def work_a():
+        wide_step(NAR, 1)
+        for t in range(1, bits):
+            gather_step(3, t)
+        z1(CON, late)
+        wide_send(EXP, 0)
+        z3(WID)
+        z2(CON, early)
+
+    narrow_cotangent(r.a1, 0, ig[0], ib[0], 7, False, work_a)
+    for t in range(2, bits + 1):
+        wide_step(NAR, t)
     wide_begin(RED, images, r.dn)
 
     out_copy.wait()
@@ -1034,37 +1083,78 @@
     lax.fori_loop(0, CHANNELS // 512, finish, 0)
     grad_copy = dma(r.obuf, r.grad_h, r.out_sem.at[1])
     grad_copy.start()
-    wide_step(EXP, 2)
     wide_core(RED)
-    z3(CON)
-    z3(NAR)
+    wide_send(RED, 0)
+    z2(CON, late)
+    z3(CON, early)
+    z2(NAR)
     gather_end(3)
     tiny_wait(1)
+    deep_make(DEF)
+    z3(CON, late)
+    z4(WID)
+    z3(NAR)
     z4(CON)
-    z_clear(CON)
-    deep_make(DEF)
+    wide_step(EXP, 1)
+    deep_core(DEF)
+    z1(OFF)
+    z1(DEF)
     wide_step(RED, 1)
-    z2(EXP)
-    deep_core(DEF)
+    for t in range(2, bits + 1):
+        wide_step(EXP, t)
     z4(NAR)
-    z_clear(NAR)
-    wide_step(RED, 2)
-    z3(EXP)
-    z4(EXP)
     z2(OFF)
     z2(DEF)
-    z2(RED)
+    for t in range(2, bits + 1):
+        wide_step(RED, t)
+    z2(EXP)
     z3(OFF)
     z3(DEF)
+    z2(RED)
+    z3(EXP)
     z3(RED)
     z4(OFF)
     z4(DEF)
+    z4(EXP)
     z4(RED)
-    for u in (EXP, OFF, DEF, RED):
+    for u in range(7):
         z_clear(u)
     grad_copy.wait()
     for tag in list(waiting):
         flush(tag)
+
+
+MOVED = ["out", "grad", "con", "def", "wid", "nar", "exp", "red"]
+
+
+def deliver(dp, names, *refs):
+    r = types.SimpleNamespace(**dict(zip(names, refs)))
+    _, _, _, deep, _ = layout(dp)
+    place = lax.axis_index("dp")
+    moves = []
+    for i, name in enumerate(MOVED):
+        source, target, hold = (getattr(r, kind + name) for kind in ("from_", "to_", "hold_"))
+        taken = pltpu.make_async_copy(source, hold, r.sems.at[0, i])
+        taken.start()
+        moves.append((taken, pltpu.make_async_copy(hold, target, r.sems.at[1, i])))
+
+    for taken, given in moves:
+        taken.wait()
+        given.start()
+
+    def span(ref, start, target):
+        rows, lanes = ref.shape
+        moved = pltpu.roll(ref[...], lax.rem(lanes - start, lanes), 1)
+        target[...] = moved[: target.shape[0], : target.shape[1]]
+
+    span(r.g_ig, place * (INNER // dp), r.to_ig)
+    span(r.g_ib, place * (INNER // dp), r.to_ib)
+    span(r.g_bg, place * (CHANNELS // dp), r.to_bg)
+    span(r.g_bb, place * (CHANNELS // dp), r.to_bb)
+    chip, core = lax.div(place, 2), lax.rem(place, 2)
+    span(r.g_off, lax.rem(2 * deep * chip, INNER) + deep * core, r.to_off)
+    for taken, given in moves:
+        given.wait()
 
 
 def per_device(
@@ -1101,7 +1191,7 @@
         images_h=(far, images.reshape(ROWS, CHANNELS)),
         cot_h=(far, cotangent.reshape(ROWS, CHANNELS)),
         red_h=(far, reducer),
-        off_h=(far, offseter),
+        off_h=(far, offseter.T),
         def_h=(far, deformer),
         exp_h=(far, expander),
         nar_h=(far, narrower),
@@ -1132,29 +1222,54 @@
         out_specs=[space for space, _ in outputs.values()],
         scratch_shapes=list(buffers.values()),
         compiler_params=pltpu.CompilerParams(
-            collective_id=0, has_side_effects=True, vmem_limit_bytes=62 * 1024 * 1024
+            collective_id=0, has_side_effects=True, vmem_limit_bytes=63 * 1024 * 1024
         ),
         name="chain",
     )(*[value for _, value in inputs.values()])
-    out, grad, g_red, g_off, g_def, g_exp, g_nar, g_con, g_wid, g_ig, g_ib, g_bg, g_bb, _ = outs
-    place = lax.axis_index("dp")
-    inner_share, broad_share = INNER // dp, CHANNELS // dp
-    begin = 2 * deep * (place // 2) % INNER + deep * (place % 2)
-    g_off = lax.dynamic_slice_in_dim(g_off.T, begin, deep, 0)[:, :OFFSETS]
+    held = dict(zip(outputs, outs))
+    big = dict(
+        out=held["out_h"],
+        grad=held["grad_h"],
+        red=held["g_red"],
+        **{"def": held["g_def"]},
+        exp=held["g_exp"],
+        nar=held["g_nar"],
+        con=held["g_con"],
+        wid=held["g_wid"],
+    )
+    small = {name: held[name] for name in ("g_off", "g_ig", "g_ib", "g_bg", "g_bb")}
+    firsts = {"from_" + name: value for name, value in big.items()}
+    finals = {"to_" + name: shape(value.shape, value.dtype) for name, value in big.items()}
+    holds = {"hold_" + name: pltpu.VMEM(value.shape, value.dtype) for name, value in big.items()}
+    lasts = dict(
+        to_off=shape((OFFSETS, deep), F32),
+        to_ig=shape((4, INNER // dp), F32),
+        to_ib=shape((4, INNER // dp), F32),
+        to_bg=shape((2, CHANNELS // dp), F32),
+        to_bb=shape((2, CHANNELS // dp), F32),
+    )
+    names = [*firsts, *small, *finals, *lasts, *holds, "sems"]
+    got = pl.pallas_call(
+        functools.partial(deliver, dp, names),
+        out_shape=[*finals.values(), *lasts.values()],
+        in_specs=[far] * len(firsts) + [vmem] * len(small),
+        out_specs=[far] * len(finals) + [vmem] * len(lasts),
+        scratch_shapes=[*holds.values(), pltpu.SemaphoreType.DMA((2, len(big)))],
+        compiler_params=pltpu.CompilerParams(vmem_limit_bytes=60 * 1024 * 1024),
+        name="deliver",
+    )(*firsts.values(), *small.values())
+    out, grad, g_red, g_def, g_exp, g_nar, g_con, g_wid, g_off, *others = got
     return (
         out.reshape(SLOTS, PIXELS, CHANNELS),
         grad.reshape(SLOTS, PIXELS, CHANNELS),
         g_red,
-        g_off,
+        g_off.T,
         g_def,
         g_exp,
         g_nar,
         g_con,
         g_wid,
-        lax.dynamic_slice_in_dim(g_ig, place * inner_share, inner_share, 1),
-        lax.dynamic_slice_in_dim(g_ib, place * inner_share, inner_share, 1),
-        lax.dynamic_slice_in_dim(g_bg, place * broad_share, broad_share, 1),
-        lax.dynamic_slice_in_dim(g_bb, place * broad_share, broad_share, 1),
+        *others,
     )
 
 

time: 383 us -> 313 us (0.82)
  Pallas kernels: 365 us -> 311 us
  local copies, waits for them, and re-layouts: 16.4 us -> 0 us
    pallas_call x1, Pallas kernels: 365 us -> 304 us  [per_device(): pl.pallas_call(functools.partial(kernel, dp, outer, names), out_shape=[sp...]
    unnamed x23 -> x0, local copies, waits for them, and re-layouts: 12.2 us -> none
    pallas_call x0 -> x1, Pallas kernels: none -> 7.33 us  [per_device(): pl.pallas_call(functools.partial(deliver, dp, names), out_shape=[*finals....]
    dynamic_slice x3 -> x0, local copies, waits for them, and re-layouts: 4.21 us -> none  [the longest x1 1.6 us: per_device(): g_off = lax.dynamic_slice_in_dim(g_off.T, begin, deep, 0)[:, :OFFSETS]]
where the time goes in v3:
time: 313 us; the launch traced here: 312 us
  Pallas kernels  311 us (99%)
    pallas_call x1, Pallas kernels, per_device(): pl.pallas_call(functools.partial(kernel, dp, outer, names), out_shape=[sp...  304 us
    pallas_call x1, Pallas kernels, per_device(): pl.pallas_call(functools.partial(deliver, dp, names), out_shape=[*finals....  7.33 us

profile of v3, /device:TPU:0, one launch (start us, length us, event | category | flops | bytes accessed | tf_op | source)
XLA Modules:
  0.0 311.7 jit_solution(13450114188344038448)
XLA Ops:
  0.7 303.7 %chain.1 = (bf16[288,2048]{1,0:T(8,128)(2,1)}, bf16[288,2048]{1,0:T(8,128)(2,1)}, f32[256,512]{1,0:T(8,128)}, f32[24,1536]{1,0:T(8,128)}, f32[576,512]{1,0:T(8,1...) custom-call(s32[32]{0:T(128)} %refs_0_.1, ...), custom_call_target="tpu_custom_call" | custom-call | tf_op jit(solution)/shard_map/chain/pallas_call | solution.py:1218
  304.3 7.3 %deliver.1 = (bf16[288,2048]{1,0:T(8,128)(2,1)}, bf16[288,2048]{1,0:T(8,128)(2,1)}, f32[256,512]{1,0:T(8,128)}, f32[576,512]{1,0:T(8,128)}, f32[256,512]{1,0:T(8...) custom-call(bf16[288,2048]{1,0:T(8,128)(2,1)} %get-tuple-element.39., ...), custom_call_target="tpu_custom_call" | custom-call | tf_op jit(solution)/shard_map/deliver/pallas_call | solution.py:1252

commit v4 on v3

--- a/solution.py
+++ b/solution.py
@@ -103,7 +103,7 @@
         taken=vmem((group, ROWS, INNER), F32),
         drawn=vmem((2, ROWS, INNER), F32),
         yall=vmem((group * ROWS, INNER), BF),
-        xall=vmem((group * ROWS, INNER), BF),
+        xall=vmem((2, group * ROWS, INNER), BF),
         grad=vmem((taps * INNER, INNER), F32),
         cored=vmem((deep, INNER), F32),
         zdeep=vmem((2, 2, deep // 2, INNER), F32),
@@ -125,6 +125,7 @@
         step_r=dma((4, 2, bits)),
         give_sem=dma((4,)),
         take_sem=dma((3,)),
+        x_sem=dma((2,)),
         ag_s=dma((4, 2, bits)),
         ag_r=dma((4, 2, bits)),
         tiny_s=dma((2,)),
@@ -464,15 +465,20 @@
     pool, land, grad, far_blocks = r.pool, r.land, r.grad, r.far_blocks
 
     deep_parts = 4 if deep % 32 == 0 else 2
+    wide_parts = {WID: 2, NAR: 2, EXP: 2, RED: 4}
+
+    def z_hold(u):
+        if u == RED:
+            return [r.a3.at[i, pl.ds(0, wide)] for i in range(3)]
+        return [r.zwide.at[nth[u], i] for i in range(3)]
 
     def z_parts(u):
         if u in nth:
-            if u == RED:
-                hold = [r.a3.at[i, pl.ds(0, wide)] for i in range(3)]
-            else:
-                hold = [r.zwide.at[nth[u], i] for i in range(3)]
-            for hs in halves:
-                yield tuple(ref.at[:, hs] for ref in hold) + (result[u].at[:, hs],)
+            hold = z_hold(u)
+            for q in range(wide_parts[u]):
+                rows = wide // (wide_parts[u] // 2)
+                rs, hs = pl.ds(q // 2 * rows, rows), halves[q % 2]
+                yield tuple(ref.at[rs, hs] for ref in hold) + (result[u].at[rs, hs],)
         elif u == OFF:
             yield r.goff, r.zoff.at[0], r.zoff.at[1], result[u]
         else:
@@ -606,7 +612,7 @@
             p, first, count, (sent, received), region = step_place(u, h, t)
             settle(region, received)
             if t == bits - 1:
-                mix(list(z_parts(u))[h][0], pool.at[p, chip, :, halves[h]], land.at[p, h, first])
+                mix(z_hold(u)[0].at[:, halves[h]], pool.at[p, chip, :, halves[h]], land.at[p, h, first])
             else:
                 for j in range(count):
                     accumulate(
@@ -696,22 +702,78 @@
     first_tap = lax.div(2 * deep * chip, INNER)
     margin = 2 * deep * chip - first_tap * INNER
 
+    def taps_of(kk):
+        k = jnp.minimum(first_tap + kk, TAPS - 1)
+        return (k, *steps_of(k))
+
+    def fetch_fields(a, g):
+        copy = dma(far_blocks.at[a, pl.ds(g * group, group)], r.taken, r.take_sem.at[2])
+        copy.start()
+        copy.wait()
+
+    def image_of(i, g):
+        m, s = lax.div(i, SLOTS), lax.rem(i, SLOTS)
+        rows = pl.ds(pl.multiple_of(i * PIXELS, PIXELS), PIXELS)
+        field = r.taken[m, pl.ds(pl.multiple_of(s * PIXELS, PIXELS), PIXELS), :].astype(BF)
+        flat = r.tiny[0, g * group + m, s, 18:19, :] == 0.0
+        dr = jnp.where(flat, r.geo[0, 0], r.geo[1, 0])
+        dc = jnp.where(flat, r.geo[0, 1], r.geo[1, 1])
+        return g * group + m, s, rows, field, dr, dc
+
+    def group_rows(g):
+        return pl.ds(g * (group * ROWS), group * ROWS)
+
+    def columns(u, kk):
+        x = 1 if u == DEF else 0
+        k, down, across = taps_of(kk)
+        for g in range(chips // group):
+            if kk == 0 or chips > group:
+                fetch_fields(0 if u == DEF else 1, g)
+            if g == 0:
+                flush("columns")
+
+            def image(i, carry):
+                m, s, rows, field, dr, dc = image_of(i, g)
+                if u == CON:
+                    hit = jnp.where((dr == down) & (dc == across), 1.0, 0.0).astype(BF)
+                    r.xall[0, rows, :] = mm(hit, field, NN).astype(BF)
+                    return carry
+                tiny = r.tiny.at[0, m, s]
+                fy, fx = tiny[pl.ds(2 * k, 1), :], tiny[pl.ds(2 * k + 1, 1), :]
+                ay = jnp.where(dr == -down, 1.0 - fy, jnp.where(dr == -down - 1, fy, 0.0))
+                ax = jnp.where(dc == -across, 1.0 - fx, jnp.where(dc == -across - 1, fx, 0.0))
+                r.xall[0, rows, :] = mm((ay * ax).astype(BF), field, TN).astype(BF)
+                return carry
+
+            lax.fori_loop(0, group * SLOTS, image, 0)
+            place = r.far_columns.at[x, kk, group_rows(g)]
+            copy = dma(r.xall.at[0], place, r.x_sem.at[0])
+            copy.start()
+            if g + 1 < chips // group:
+                copy.wait()
+            else:
+                later("columns", place, r.x_sem.at[0])
+
     def deep_make(u):
         flush("deep")
-        field_of, back_of = (0, 3) if u == DEF else (1, 2)
+        flush("columns")
+        x, back_of = (1, 3) if u == DEF else (0, 2)
         for g in range(chips // group):
-            fields = dma(
-                far_blocks.at[field_of, pl.ds(g * group, group)], r.taken, r.take_sem.at[2]
-            )
-            fields.start()
 
             def fetch(m):
                 return dma(
                     far_blocks.at[back_of, g * group + m], r.drawn.at[m % 2], r.take_sem.at[m % 2]
                 )
 
+            def draw(kk):
+                slot = lax.rem(kk, 2)
+                return dma(
+                    r.far_columns.at[x, kk, group_rows(g)], r.xall.at[slot], r.x_sem.at[slot]
+                )
+
             for m in range(min(2, group)):
                 fetch(m).start()
+            draw(0).start()
             for m in range(group):
                 fetch(m).wait()
 
@@ -724,56 +786,54 @@
                 lax.fori_loop(0, ROWS // 32, lower, 0)
                 if m + 2 < group:
                     fetch(m + 2).start()
-            fields.wait()
 
             def one(kk, carry):
-                k = jnp.minimum(first_tap + kk, TAPS - 1)
-                down, across = steps_of(k)
-
-                def image(i, share):
-                    m, s = lax.div(i, SLOTS), lax.rem(i, SLOTS)
-                    rows = pl.ds(pl.multiple_of(i * PIXELS, PIXELS), PIXELS)
-                    there = pl.ds(pl.multiple_of(s * PIXELS, PIXELS), PIXELS)
-                    field = r.taken[m, there, :].astype(BF)
-                    tiny = r.tiny.at[0, g * group + m, s]
-                    flat = tiny[18:19, :] == 0.0
-                    dr = jnp.where(flat, r.geo[0, 0], r.geo[1, 0])
-                    dc = jnp.where(flat, r.geo[0, 1], r.geo[1, 1])
-                    hit = jnp.where((dr == down) & (dc == across), 1.0, 0.0).astype(BF)
-                    if u == CON:
-                        r.xall[rows, :] = mm(hit, field, NN).astype(BF)
-                        return share
-                    fy, fx = tiny[pl.ds(2 * k, 1), :], tiny[pl.ds(2 * k + 1, 1), :]
-                    ay = jnp.where(dr == -down, 1.0 - fy, jnp.where(dr == -down - 1, fy, 0.0))
-                    ax = jnp.where(
-                        dc == -across, 1.0 - fx, jnp.where(dc == -across - 1, fx, 0.0)
-                    )
-                    r.xall[rows, :] = mm((ay * ax).astype(BF), field, TN).astype(BF)
-                    shift = r.tiny[1, g * group + m, s].astype(BF)
-                    moved = mm(shift, hit, NN).astype(BF)
-                    return share + mm(moved, field, NN)
-
+                @pl.when(kk + 1 < taps)
+                def _():
+                    draw(kk + 1).start()
+
+                draw(kk).wait()
                 at = pl.ds(pl.multiple_of(kk * INNER, INNER), INNER)
-                zero = jnp.zeros((24, INNER) if u == DEF else (8, 128), F32)
-                share = lax.fori_loop(0, group * SLOTS, image, zero)
-                part = mm(r.xall[...], r.yall[...], TN)
+                part = mm(r.xall[lax.rem(kk, 2)], r.yall[...], TN)
                 if g == 0:
                     grad[at, :] = part
                 else:
                     grad[at, :] += part
-                if u == DEF:
-                    if g == 0:
-                        r.goff[:, at] = share
-                    else:
-                        r.goff[:, at] += share
                 return carry
 
             lax.fori_loop(0, taps, one, 0)
         away = pl.ds(pl.multiple_of(margin + (1 - core) * deep, 8), deep)
         send(grad.at[away], r.cored, r.core_s.at[u], r.core_r.at[u], sibling)
         later("deep", r.cored, r.core_s.at[u])
-        if u == DEF:
-            send(r.goff, r.coreo, r.core_s.at[OFF], r.core_r.at[OFF], sibling)
+
+    def off_make():
+        for g in range(chips // group):
+            fetch_fields(0, g)
+
+            def one(kk, carry):
+                k, down, across = taps_of(kk)
+
+                def image(i, share):
+                    m, s, rows, field, dr, dc = image_of(i, g)
+                    hit = jnp.where((dr == down) & (dc == across), 1.0, 0.0).astype(BF)
+                    moved = mm(r.tiny[1, m, s].astype(BF), hit, NN).astype(BF)
+                    return share + mm(moved, field, NN)
+
+                at = pl.ds(pl.multiple_of(kk * INNER, INNER), INNER)
+                share = lax.fori_loop(0, group * SLOTS, image, jnp.zeros((24, INNER), F32))
+                if g == 0:
+                    r.goff[:, at] = share
+                else:
+                    r.goff[:, at] += share
+                return carry
+
+            lax.fori_loop(0, taps, one, 0)
+        send(r.goff, r.coreo, r.core_s.at[OFF], r.core_r.at[OFF], sibling)
+
+    def off_core():
+        settle(r.goff, r.core_s.at[OFF])
+        settle(r.coreo, r.core_r.at[OFF])
+        accumulate(r.goff, r.coreo)
 
     def deep_core(u):
         settle(r.cored, r.core_r.at[u])
@@ -789,11 +849,6 @@
                 return carry
 
             lax.fori_loop(0, half // step, body, 0)
-        if u == DEF:
-            settle(r.goff, r.core_s.at[OFF])
-            settle(r.coreo, r.core_r.at[OFF])
-            accumulate(r.goff, r.coreo)
-
     images, between, acc, up = r.images, r.between, r.acc, r.up
     ig = [r.ig[i : i + 1, :] for i in range(4)]
     ib = [r.ib[i : i + 1, :] for i in range(4)]
@@ -917,6 +972,7 @@
     def work_b1():
         gather_end(0)
         tiny_wait(0)
+        columns(DEF, 0)
 
     narrow_stats(r.b1, 2, work_b1)
     norm_silu(r.b1, 2, ig[2], ib[2], r.narrow, True)
@@ -935,12 +991,22 @@
 
     lax.fori_loop(0, TAPS, convolve, 0)
     r.b2[...] = acc[...]
-    narrow_stats(r.b2, 3, lambda: gather_first(1, 1))
+    def work_b2():
+        gather_first(1, 1)
+        columns(DEF, 1)
+
+    narrow_stats(r.b2, 3, work_b2)
     norm_silu(r.b2, 3, ig[3], ib[3], r.mixed, False)
 
     loads.wid_h.wait()
     widen(r.mixed, r.redwid, r.b3)
-    wide_stats(r.b3, 1, lambda: gather_rest(1))
+
+    def work_b3():
+        gather_rest(1)
+        for kk in range(2, taps):
+            columns(DEF, kk)
+
+    wide_stats(r.b3, 1, work_b3)
 
     loads.cot_h.wait()
 
@@ -950,16 +1016,23 @@
         r.obuf[rs, cs] = (lv * (z * sg)).astype(BF)
         return r.dwide[rs, cs].astype(F32) * (lv * (sg * (1.0 + z * (1.0 - sg))))
 
-    wide_cotangent(
-        2, r.b3, 1, bg[1], bb[1], last, nothing, lambda: gather_end(1)
-    )
+    def work_f():
+        gather_end(1)
+        columns(CON, 0)
+
+    wide_cotangent(2, r.b3, 1, bg[1], bb[1], last, nothing, work_f)
     out_copy = dma(r.obuf, r.out_h, r.out_sem.at[0])
     out_copy.start()
     wide_begin(WID, r.dwide, r.mixed)
     acc[...] = mm(r.dwide[...], r.redwid[...], NN)
     loads.red_h = load(9, r.red_h, r.redwid)
     wide_core(WID)
-    narrow_cotangent(r.b2, 3, ig[3], ib[3], 4, True, lambda: wide_send(WID, 0))
+
+    def work_e():
+        wide_send(WID, 0)
+        columns(CON, 1)
+
+    narrow_cotangent(r.b2, 3, ig[3], ib[3], 4, True, work_e)
 
     acc[...] = jnp.zeros((ROWS, INNER), F32)
 
@@ -975,10 +1048,14 @@
     loads.def_h = load(10, r.def_h, r.dfmcon)
 
     def work_d():
+        wide_step(WID, 1)
         gather_start(2)
-        wide_step(WID, 1)
+        for kk in range(2, taps):
+            columns(CON, kk)
 
     narrow_cotangent(r.b1, 2, ig[2], ib[2], 5, False, work_d)
+    for t in range(2, bits + 1):
+        wide_step(WID, t)
     wide_begin(NAR, between, r.dn)
 
     def add_back(n, carry):
@@ -999,8 +1076,7 @@
             gather_step(2, t)
 
     def work_more_c():
-        for t in range(2, bits + 1):
-            wide_step(WID, t)
+        z2(WID)
 
     wide_cotangent(3, r.a3, 0, bg[0], bb[0], first, work_c, work_more_c)
     wide_begin(EXP, r.dwide, r.hidden)
@@ -1009,11 +1085,12 @@
 
     def work_b():
         wide_send(NAR, 0)
-        z2(WID)
+        z3(WID)
         gather_end(2)
         deep_make(CON)
 
     narrow_cotangent(r.a2, 1, ig[1], ib[1], 6, True, work_b)
+    wide_step(NAR, 1)
     gather_start(3)
     deep_core(CON)
     early, late = range(deep_parts // 2), range(deep_parts // 2, deep_parts)
@@ -1059,17 +1136,16 @@
     lax.fori_loop(0, TAPS, untap, 0)
 
     def work_a():
-        wide_step(NAR, 1)
         for t in range(1, bits):
             gather_step(3, t)
+        wide_send(EXP, 0)
         z1(CON, late)
-        wide_send(EXP, 0)
-        z3(WID)
+        for t in range(2, bits + 1):
+            wide_step(NAR, t)
         z2(CON, early)
+        z4(WID)
 
     narrow_cotangent(r.a1, 0, ig[0], ib[0], 7, False, work_a)
-    for t in range(2, bits + 1):
-        wide_step(NAR, t)
     wide_begin(RED, images, r.dn)
 
     out_copy.wait()
@@ -1085,36 +1161,42 @@
     grad_copy.start()
     wide_core(RED)
     wide_send(RED, 0)
+    gather_end(3)
+    deep_make(DEF)
     z2(CON, late)
     z3(CON, early)
+    deep_core(DEF)
+    z1(DEF)
+    tiny_wait(1)
+    off_make()
+    wide_step(EXP, 1)
     z2(NAR)
-    gather_end(3)
-    tiny_wait(1)
-    deep_make(DEF)
+    off_core()
+    z1(OFF)
+    z2(DEF, [0])
     z3(CON, late)
-    z4(WID)
-    z3(NAR)
-    z4(CON)
-    wide_step(EXP, 1)
-    deep_core(DEF)
-    z1(OFF)
-    z1(DEF)
     wide_step(RED, 1)
+    z2(DEF, [1])
+    z3(DEF, [0])
     for t in range(2, bits + 1):
         wide_step(EXP, t)
-    z4(NAR)
-    z2(OFF)
-    z2(DEF)
+    z2(DEF, [2])
+    z3(NAR)
     for t in range(2, bits + 1):
         wide_step(RED, t)
+    z2(DEF, [3])
+    z3(DEF, [1, 2])
+    z2(OFF)
     z2(EXP)
+    z3(DEF, [3])
     z3(OFF)
-    z3(DEF)
     z2(RED)
     z3(EXP)
     z3(RED)
+    z4(CON)
+    z4(NAR)
+    z4(DEF)
     z4(OFF)
-    z4(DEF)
     z4(EXP)
     z4(RED)
     for u in range(7):
@@ -1213,6 +1295,7 @@
         g_bg=(vmem, shape((2, CHANNELS), F32)),
         g_bb=(vmem, shape((2, CHANNELS), F32)),
         far_blocks=(far, shape((4, chips, ROWS, INNER), F32)),
+        far_columns=(far, shape((2, taps, chips * ROWS, INNER), BF)),
     )
     names = list(inputs) + list(outputs) + list(buffers)
     outs = pl.pallas_call(

time: 313 us -> 289 us (0.923)
  Pallas kernels: 311 us -> 287 us
    pallas_call x1, Pallas kernels: 304 us -> 280 us  [per_device(): pl.pallas_call(functools.partial(kernel, dp, outer, names), out_shape=[sp...]
where the time goes in v4:
time: 289 us; the launch traced here: 288 us
  Pallas kernels  287 us (99%)
    pallas_call x1, Pallas kernels, per_device(): pl.pallas_call(functools.partial(kernel, dp, outer, names), out_shape=[sp...  280 us
    pallas_call x1, Pallas kernels, per_device(): pl.pallas_call(functools.partial(deliver, dp, names), out_shape=[*finals....  7.33 us

profile of v4, /device:TPU:0, one launch (start us, length us, event | category | flops | bytes accessed | tf_op | source)
XLA Modules:
  0.0 288.1 jit_solution(12843159820475633592)
XLA Ops:
  0.7 280.0 %chain.1 = (bf16[288,2048]{1,0:T(8,128)(2,1)}, bf16[288,2048]{1,0:T(8,128)(2,1)}, f32[256,512]{1,0:T(8,128)}, f32[24,1536]{1,0:T(8,128)}, f32[576,512]{1,0:T(8,1...) custom-call(s32[32]{0:T(128)} %refs_0_.1, ...), custom_call_target="tpu_custom_call" | custom-call | tf_op jit(solution)/shard_map/chain/pallas_call | solution.py:1301
  280.6 7.3 %deliver.1 = (bf16[288,2048]{1,0:T(8,128)(2,1)}, bf16[288,2048]{1,0:T(8,128)(2,1)}, f32[256,512]{1,0:T(8,128)}, f32[576,512]{1,0:T(8,128)}, f32[256,512]{1,0:T(8...) custom-call(bf16[288,2048]{1,0:T(8,128)(2,1)} %get-tuple-element.39., ...), custom_call_target="tpu_custom_call" | custom-call | tf_op jit(solution)/shard_map/deliver/pallas_call | solution.py:1335

commit v5 on v4

--- a/solution.py
+++ b/solution.py
@@ -101,7 +101,7 @@
         tiny=vmem((2, chips, SLOTS, 24, PIXELS), F32),
         give=vmem((ROWS, INNER), F32),
         taken=vmem((group, ROWS, INNER), F32),
-        drawn=vmem((2, ROWS, INNER), F32),
+        drawn=vmem((ROWS, INNER), F32),
         yall=vmem((group * ROWS, INNER), BF),
         xall=vmem((2, group * ROWS, INNER), BF),
         grad=vmem((taps * INNER, INNER), F32),
@@ -112,6 +112,7 @@
         zoff=vmem((2, 24, taps * INNER), F32),
         free=pltpu.SemaphoreType.REGULAR,
         credit=pltpu.SemaphoreType.REGULAR((2, bits)),
+        swapped=pltpu.SemaphoreType.REGULAR,
         load_sem=dma((11,)),
         out_sem=dma((2,)),
         res_sem=dma((7, 4)),
@@ -290,10 +291,20 @@
         rx = r.rxn.at[number]
 
         def step(i, carry):
-            send(rx.at[own], rx.at[own], r.xn_s.at[number], r.xn_r.at[number], other(i))
+            line, part = lax.div(i, dp), lax.rem(i, dp)
+            z = jnp.where(mine < outer // 2, outer - 1 - line, line)
+            peer = 0
+            for bit in range(bits + 1):
+                here, turn = bit_of(me, bit), 1 - bit_of(part, bit)
+                peer = peer + (here + turn - 2 * here * turn) * (1 << bit)
+
+            @pl.when(peer * outer + z != own)
+            def _():
+                send(rx.at[own], rx.at[own], r.xn_s.at[number], r.xn_r.at[number], (peer, z))
+
             return carry
 
-        lax.fori_loop(1, everyone, step, 0)
+        lax.fori_loop(0, everyone, step, 0)
         rest = rx.at[pl.ds(0, everyone - 1)]
         later("end", rest, r.xn_s.at[number])
         work()
@@ -560,6 +571,8 @@
         flush(("keep", p))
         low = p + (2 - p) * core
         high = p + (2 - p) * (1 - core)
+        if u == EXP:
+            pl.semaphore_wait(r.swapped, 1)
 
         def step(m, carry):
             block = left[:, pl.ds(pl.multiple_of(m * (2 * wide), 2 * wide), 2 * wide)]
@@ -635,6 +648,8 @@
             return carry
 
         lax.fori_loop(0, chips, step, 0)
+        if u == NAR:
+            pl.semaphore_signal(r.swapped, inc=1, device_id=sibling, device_id_type=MESH)
 
     def wide_step(u, t):
         wide_add(u, t - 1)
@@ -745,7 +760,7 @@
                 r.xall[0, rows, :] = mm((ay * ax).astype(BF), field, TN).astype(BF)
                 return carry
 
-            lax.fori_loop(0, group * SLOTS, image, 0)
+            lax.fori_loop(0, group * SLOTS, image, 0, unroll=4)
             place = r.far_columns.at[x, kk, group_rows(g)]
             copy = dma(r.xall.at[0], place, r.x_sem.at[0])
             copy.start()
@@ -758,12 +773,11 @@
         flush("deep")
         flush("columns")
         x, back_of = (1, 3) if u == DEF else (0, 2)
+        slots = (r.give, r.drawn)
         for g in range(chips // group):
 
             def fetch(m):
-                return dma(
-                    far_blocks.at[back_of, g * group + m], r.drawn.at[m % 2], r.take_sem.at[m % 2]
-                )
+                return dma(far_blocks.at[back_of, g * group + m], slots[m % 2], r.take_sem.at[m % 2])
 
             def draw(kk):
                 slot = lax.rem(kk, 2)
@@ -780,7 +794,7 @@
                 def lower(i, carry):
                     rows = pl.ds(pl.multiple_of(m * ROWS + i * 32, 32), 32)
                     there = pl.ds(pl.multiple_of(i * 32, 32), 32)
-                    r.yall[rows, :] = r.drawn[m % 2, there, :].astype(BF)
+                    r.yall[rows, :] = slots[m % 2][there, :].astype(BF)
                     return carry
 
                 lax.fori_loop(0, ROWS // 32, lower, 0)
@@ -820,7 +834,9 @@
                     return share + mm(moved, field, NN)
 
                 at = pl.ds(pl.multiple_of(kk * INNER, INNER), INNER)
-                share = lax.fori_loop(0, group * SLOTS, image, jnp.zeros((24, INNER), F32))
+                share = lax.fori_loop(
+                    0, group * SLOTS, image, jnp.zeros((24, INNER), F32), unroll=8
+                )
                 if g == 0:
                     r.goff[:, at] = share
                 else:
@@ -896,14 +912,16 @@
     loads.off_h.wait()
     inner = r.inner
     lane = lax.broadcasted_iota(jnp.int32, (PIXELS, OFFSETS), 1)
+
+    def gather(k, carry):
+        cols = [mm(shifted(s, k), inner[slot_rows(s), :], NN).astype(BF) for s in range(SLOTS)]
+        weight = offset_tap(k)
+        return tuple(old + mm(col, weight, NT) for old, col in zip(carry, cols))
+
+    zero = jnp.zeros((PIXELS, OFFSETS), F32)
+    both_offsets = lax.fori_loop(0, TAPS, gather, (zero,) * SLOTS, unroll=3)
     for s in range(SLOTS):
-
-        def gather(k, carry):
-            col = mm(shifted(s, k), inner[slot_rows(s), :], NN).astype(BF)
-            return carry + mm(col, offset_tap(k), NT)
-
-        offsets = lax.fori_loop(0, TAPS, gather, jnp.zeros((PIXELS, OFFSETS), F32))
-        frac = sigmoid(offsets)
+        frac = sigmoid(both_offsets[s])
         r.frac[slot_rows(s), :] = frac
         coarse = frac.astype(BF)
         fine = (frac - coarse.astype(F32)).astype(BF)
@@ -937,7 +955,7 @@
         acc[...] += mm(r.turned[...], tap(r.dfmcon, k), NN)
         return carry
 
-    lax.fori_loop(0, TAPS, sample, 0)
+    lax.fori_loop(0, TAPS, sample, 0, unroll=3)
     loads.con_h = load(8, r.con_h, r.dfmcon)
     r.a2[...] = acc[...]
     narrow_stats(r.a2, 1, lambda: gather_first(0, 1))
@@ -989,7 +1007,7 @@
         acc[...] += mm(r.turned[...], tap(r.dfmcon, k), NN)
         return carry
 
-    lax.fori_loop(0, TAPS, convolve, 0)
+    lax.fori_loop(0, TAPS, convolve, 0, unroll=3)
     r.b2[...] = acc[...]
     def work_b2():
         gather_first(1, 1)
@@ -1026,9 +1044,9 @@
     wide_begin(WID, r.dwide, r.mixed)
     acc[...] = mm(r.dwide[...], r.redwid[...], NN)
     loads.red_h = load(9, r.red_h, r.redwid)
-    wide_core(WID)
 
     def work_e():
+        wide_core(WID)
         wide_send(WID, 0)
         columns(CON, 1)
 
@@ -1044,7 +1062,7 @@
         acc[...] += mm(r.turned[...], tap(r.dfmcon, k), NT)
         return carry
 
-    lax.fori_loop(0, TAPS, spread, 0)
+    lax.fori_loop(0, TAPS, spread, 0, unroll=3)
     loads.def_h = load(10, r.def_h, r.dfmcon)
 
     def work_d():
@@ -1056,7 +1074,6 @@
     narrow_cotangent(r.b1, 2, ig[2], ib[2], 5, False, work_d)
     for t in range(2, bits + 1):
         wide_step(WID, t)
-    wide_begin(NAR, between, r.dn)
 
     def add_back(n, carry):
         rows = pl.ds(pl.multiple_of(n * 512, 512), 512)
@@ -1064,7 +1081,6 @@
         return carry
 
     lax.fori_loop(0, CHANNELS // 512, add_back, 0)
-    wide_core(NAR)
 
     def first(n, rs, cs, lv, pre):
         z = pre + images[rs, cs].astype(F32)
@@ -1074,18 +1090,19 @@
     def work_c():
         for t in range(1, bits):
             gather_step(2, t)
+        wide_begin(NAR, between, r.dn)
 
     def work_more_c():
         z2(WID)
+        wide_core(NAR)
 
     wide_cotangent(3, r.a3, 0, bg[0], bb[0], first, work_c, work_more_c)
-    wide_begin(EXP, r.dwide, r.hidden)
     acc[...] = mm(r.dwide[...], r.exp[...], NN)
-    wide_core(EXP)
 
     def work_b():
         wide_send(NAR, 0)
         z3(WID)
+        wide_begin(EXP, r.dwide, r.hidden)
         gather_end(2)
         deep_make(CON)
 
@@ -1117,7 +1134,7 @@
             acc[rs, :] += mm(r.wmat[s, k], back, TN)
         return carry
 
-    lax.fori_loop(0, TAPS, unsample, 0)
+    lax.fori_loop(0, TAPS, unsample, 0, unroll=3)
     for s in range(SLOTS):
         put = r.tiny.at[1, chip, s]
         put[...] = jnp.zeros((24, PIXELS), F32)
@@ -1133,7 +1150,9 @@
             acc[rs, :] += mm(moved, offset_tap(k), NN)
         return carry
 
-    lax.fori_loop(0, TAPS, untap, 0)
+    lax.fori_loop(0, TAPS, untap, 0, unroll=3)
+
+    wide_core(EXP)
 
     def work_a():
         for t in range(1, bits):
@@ -1159,40 +1178,47 @@
     lax.fori_loop(0, CHANNELS // 512, finish, 0)
     grad_copy = dma(r.obuf, r.grad_h, r.out_sem.at[1])
     grad_copy.start()
+    gather_end(3)
+    deep_make(DEF)
     wide_core(RED)
     wide_send(RED, 0)
-    gather_end(3)
-    deep_make(DEF)
     z2(CON, late)
     z3(CON, early)
     deep_core(DEF)
     z1(DEF)
+    wide_step(EXP, 1)
+    z2(NAR)
+    z3(CON, late)
     tiny_wait(1)
     off_make()
-    wide_step(EXP, 1)
-    z2(NAR)
+    z2(DEF, [0])
     off_core()
     z1(OFF)
-    z2(DEF, [0])
-    z3(CON, late)
     wide_step(RED, 1)
     z2(DEF, [1])
-    z3(DEF, [0])
+    z3(NAR)
     for t in range(2, bits + 1):
         wide_step(EXP, t)
     z2(DEF, [2])
-    z3(NAR)
+    z3(DEF, [0])
     for t in range(2, bits + 1):
         wide_step(RED, t)
     z2(DEF, [3])
-    z3(DEF, [1, 2])
+    z3(DEF, [1])
     z2(OFF)
-    z2(EXP)
+    z2(EXP, [0])
+    z3(DEF, [2])
+    z2(EXP, [1])
     z3(DEF, [3])
     z3(OFF)
-    z2(RED)
-    z3(EXP)
-    z3(RED)
+    z3(EXP, [0])
+    z2(RED, [0])
+    z2(RED, [1])
+    z3(EXP, [1])
+    z2(RED, [2])
+    z3(RED, [0])
+    z2(RED, [3])
+    z3(RED, [1, 2, 3])
     z4(CON)
     z4(NAR)
     z4(DEF)

time: 289 us -> 273 us (0.945)
  Pallas kernels: 287 us -> 272 us
    pallas_call x1, Pallas kernels: 280 us -> 265 us  [per_device(): pl.pallas_call(functools.partial(kernel, dp, outer, names), out_shape=[sp...]
where the time goes in v5:
time: 273 us
  Pallas kernels  272 us (100%)
    pallas_call x1, Pallas kernels, per_device(): pl.pallas_call(functools.partial(kernel, dp, outer, names), out_shape=[sp...  265 us
    pallas_call x1, Pallas kernels, per_device(): pl.pallas_call(functools.partial(deliver, dp, names), out_shape=[*finals....  7.33 us

profile of v5, /device:TPU:0, one launch (start us, length us, event | category | flops | bytes accessed | tf_op | source)
XLA Modules:
  0.0 272.9 jit_solution(1285818465185443912)
XLA Ops:
  0.7 264.8 %chain.1 = (bf16[288,2048]{1,0:T(8,128)(2,1)}, bf16[288,2048]{1,0:T(8,128)(2,1)}, f32[256,512]{1,0:T(8,128)}, f32[24,1536]{1,0:T(8,128)}, f32[576,512]{1,0:T(8,1...) custom-call(s32[32]{0:T(128)} %refs_0_.1, ...), custom_call_target="tpu_custom_call" | custom-call | tf_op jit(solution)/shard_map/chain/pallas_call | solution.py:1327
  265.5 7.3 %deliver.1 = (bf16[288,2048]{1,0:T(8,128)(2,1)}, bf16[288,2048]{1,0:T(8,128)(2,1)}, f32[256,512]{1,0:T(8,128)}, f32[576,512]{1,0:T(8,128)}, f32[256,512]{1,0:T(8...) custom-call(bf16[288,2048]{1,0:T(8,128)(2,1)} %get-tuple-element.39., ...), custom_call_target="tpu_custom_call" | custom-call | tf_op jit(solution)/shard_map/deliver/pallas_call | solution.py:1361

commit v6 on v5

--- a/solution.py
+++ b/solution.py
@@ -1135,6 +1135,7 @@
         return carry
 
     lax.fori_loop(0, TAPS, unsample, 0, unroll=3)
+    z2(CON, [0])
     for s in range(SLOTS):
         put = r.tiny.at[1, chip, s]
         put[...] = jnp.zeros((24, PIXELS), F32)
@@ -1161,12 +1162,13 @@
         z1(CON, late)
         for t in range(2, bits + 1):
             wide_step(NAR, t)
-        z2(CON, early)
+        z2(CON, [1])
         z4(WID)
 
     narrow_cotangent(r.a1, 0, ig[0], ib[0], 7, False, work_a)
+    z3(CON, [0])
     wide_begin(RED, images, r.dn)
-
+    z2(CON, [2])
     out_copy.wait()
     loads.red_h.wait()
 
@@ -1178,25 +1180,28 @@
     lax.fori_loop(0, CHANNELS // 512, finish, 0)
     grad_copy = dma(r.obuf, r.grad_h, r.out_sem.at[1])
     grad_copy.start()
+    z2(CON, [3])
+    z3(CON, [1])
     gather_end(3)
     deep_make(DEF)
+    z2(NAR, [0])
+    z3(CON, [2])
     wide_core(RED)
     wide_send(RED, 0)
-    z2(CON, late)
-    z3(CON, early)
     deep_core(DEF)
     z1(DEF)
+    z2(NAR, [1])
+    z3(CON, [3])
     wide_step(EXP, 1)
-    z2(NAR)
-    z3(CON, late)
     tiny_wait(1)
     off_make()
     z2(DEF, [0])
+    z3(NAR, [0])
     off_core()
     z1(OFF)
     wide_step(RED, 1)
     z2(DEF, [1])
-    z3(NAR)
+    z3(NAR, [1])
     for t in range(2, bits + 1):
         wide_step(EXP, t)
     z2(DEF, [2])
@@ -1206,19 +1211,21 @@
     z2(DEF, [3])
     z3(DEF, [1])
     z2(OFF)
+    z3(DEF, [2])
     z2(EXP, [0])
-    z3(DEF, [2])
-    z2(EXP, [1])
     z3(DEF, [3])
     z3(OFF)
+    z2(EXP, [1])
+    z2(RED, [0])
     z3(EXP, [0])
-    z2(RED, [0])
     z2(RED, [1])
+    z2(RED, [2])
     z3(EXP, [1])
-    z2(RED, [2])
+    z2(RED, [3])
     z3(RED, [0])
-    z2(RED, [3])
-    z3(RED, [1, 2, 3])
+    z3(RED, [1])
+    z3(RED, [2])
+    z3(RED, [3])
     z4(CON)
     z4(NAR)
     z4(DEF)

time: 273 us -> 262 us (0.960)
  Pallas kernels: 272 us -> 261 us
    pallas_call x1, Pallas kernels: 265 us -> 253 us  [per_device(): pl.pallas_call(functools.partial(kernel, dp, outer, names), out_shape=[sp...]
where the time goes in v6:
time: 262 us
  Pallas kernels  261 us (100%)
    pallas_call x1, Pallas kernels, per_device(): pl.pallas_call(functools.partial(kernel, dp, outer, names), out_shape=[sp...  253 us
    pallas_call x1, Pallas kernels, per_device(): pl.pallas_call(functools.partial(deliver, dp, names), out_shape=[*finals....  7.33 us

profile of v6, /device:TPU:0, one launch (start us, length us, event | category | flops | bytes accessed | tf_op | source)
XLA Modules:
  0.0 261.6 jit_solution(5242962385741570270)
XLA Ops:
  0.7 253.4 %chain.1 = (bf16[288,2048]{1,0:T(8,128)(2,1)}, bf16[288,2048]{1,0:T(8,128)(2,1)}, f32[256,512]{1,0:T(8,128)}, f32[24,1536]{1,0:T(8,128)}, f32[576,512]{1,0:T(8,1...) custom-call(s32[32]{0:T(128)} %refs_0_.1, ...), custom_call_target="tpu_custom_call" | custom-call | tf_op jit(solution)/shard_map/chain/pallas_call | solution.py:1334
  254.1 7.3 %deliver.1 = (bf16[288,2048]{1,0:T(8,128)(2,1)}, bf16[288,2048]{1,0:T(8,128)(2,1)}, f32[256,512]{1,0:T(8,128)}, f32[576,512]{1,0:T(8,128)}, f32[256,512]{1,0:T(8...) custom-call(bf16[288,2048]{1,0:T(8,128)(2,1)} %get-tuple-element.39., ...), custom_call_target="tpu_custom_call" | custom-call | tf_op jit(solution)/shard_map/deliver/pallas_call | solution.py:1368

commit v7 on v6

--- a/solution.py
+++ b/solution.py
@@ -212,7 +212,7 @@
                 carry = body(pl.ds(pl.multiple_of(i * 48 + j * 16, 16), 16), lv, carry)
             return carry
 
-        return lax.fori_loop(0, 6, step, init)
+        return lax.fori_loop(0, 6, step, init, unroll=2)
 
     def send(source, target, sent, received, device):
         pltpu.make_async_remote_copy(
@@ -313,27 +313,30 @@
 
     def share_wide(number, forward, work, work_more):
         rx1, rx2 = r.rxw1.at[number], r.rxw2.at[number]
-        for step in range(1, dp):
-            send(
-                rx1.at[me],
-                rx1.at[me],
-                r.xw_s.at[number, 0],
-                r.xw_r.at[number, 0],
-                (lax.rem(me + step, dp), mine),
-            )
+        for turn in range(dp - 1, 0, -1):
+            peer = me
+            for bit in range(bits + 1):
+                if (turn >> bit) & 1:
+                    peer = flip(peer, bit)
+            send(rx1.at[me], rx1.at[me], r.xw_s.at[number, 0], r.xw_r.at[number, 0], (peer, mine))
         rest = rx1.at[pl.ds(0, dp - 1)]
         later("end", rest, r.xw_s.at[number, 0])
         work()
         settle(rest, r.xw_r.at[number, 0])
         rx2[mine] = merge(rx1, near, near_total, forward)
-        for step in range(1, outer):
-            send(
-                rx2.at[mine],
-                rx2.at[mine],
-                r.xw_s.at[number, 1],
-                r.xw_r.at[number, 1],
-                (me, lax.rem(mine + step, outer)),
-            )
+        for line in range(outer):
+            z = jnp.where(mine < outer // 2, outer - 1 - line, line)
+
+            @pl.when(z != mine)
+            def _():
+                send(
+                    rx2.at[mine],
+                    rx2.at[mine],
+                    r.xw_s.at[number, 1],
+                    r.xw_r.at[number, 1],
+                    (me, z),
+                )
+
         rest = rx2.at[pl.ds(0, outer - 1)]
         later("end", rest, r.xw_s.at[number, 1])
         work_more()
@@ -967,7 +970,7 @@
             target[n] = mm(source[...], weight[rows, :], NT)
             return carry
 
-        lax.fori_loop(0, CHANNELS // 512, step, 0)
+        lax.fori_loop(0, CHANNELS // 512, step, 0, unroll=2)
 
     loads.exp_h.wait()
     widen(r.hidden, r.exp, r.a3)
@@ -1080,7 +1083,7 @@
         up[n] += mm(r.dn[...], r.nar[rows, :], NT)
         return carry
 
-    lax.fori_loop(0, CHANNELS // 512, add_back, 0)
+    lax.fori_loop(0, CHANNELS // 512, add_back, 0, unroll=2)
 
     def first(n, rs, cs, lv, pre):
         z = pre + images[rs, cs].astype(F32)
@@ -1177,7 +1180,7 @@
         r.obuf[:, rows] = (up[n] + mm(r.dn[...], r.redwid[rows, :], NT)).astype(BF)
         return carry
 
-    lax.fori_loop(0, CHANNELS // 512, finish, 0)
+    lax.fori_loop(0, CHANNELS // 512, finish, 0, unroll=2)
     grad_copy = dma(r.obuf, r.grad_h, r.out_sem.at[1])
     grad_copy.start()
     z2(CON, [3])

time: 262 us -> 260 us (level)
  Pallas kernels: 261 us -> 257 us
    pallas_call x1, Pallas kernels: 253 us -> 250 us  [per_device(): pl.pallas_call(functools.partial(kernel, dp, outer, names), out_shape=[sp...]
where the time goes in v7:
time: 260 us; the launch traced here: 258 us
  Pallas kernels  257 us (99%)
    pallas_call x1, Pallas kernels, per_device(): pl.pallas_call(functools.partial(kernel, dp, outer, names), out_shape=[sp...  250 us
    pallas_call x1, Pallas kernels, per_device(): pl.pallas_call(functools.partial(deliver, dp, names), out_shape=[*finals....  7.33 us

profile of v7, /device:TPU:0, one launch (start us, length us, event | category | flops | bytes accessed | tf_op | source)
XLA Modules:
  0.0 257.9 jit_solution(9681892954851638525)
XLA Ops:
  0.7 249.8 %chain.1 = (bf16[288,2048]{1,0:T(8,128)(2,1)}, bf16[288,2048]{1,0:T(8,128)(2,1)}, f32[256,512]{1,0:T(8,128)}, f32[24,1536]{1,0:T(8,128)}, f32[576,512]{1,0:T(8,1...) custom-call(s32[32]{0:T(128)} %refs_0_.1, ...), custom_call_target="tpu_custom_call" | custom-call | tf_op jit(solution)/shard_map/chain/pallas_call | solution.py:1337
  250.4 7.3 %deliver.1 = (bf16[288,2048]{1,0:T(8,128)(2,1)}, bf16[288,2048]{1,0:T(8,128)(2,1)}, f32[256,512]{1,0:T(8,128)}, f32[576,512]{1,0:T(8,128)}, f32[256,512]{1,0:T(8...) custom-call(bf16[288,2048]{1,0:T(8,128)(2,1)} %get-tuple-element.39., ...), custom_call_target="tpu_custom_call" | custom-call | tf_op jit(solution)/shard_map/deliver/pallas_call | solution.py:1371

commit v8 on v7

--- a/solution.py
+++ b/solution.py
@@ -248,7 +248,8 @@
             target[rs, :] += source[rs, :]
             return carry
 
-        lax.fori_loop(0, rows // step, body, 0)
+        count = rows // step
+        lax.fori_loop(0, count, body, 0, unroll=math.gcd(count, 3) if count % 2 else 2)
 
     def mix(target, one, two):
         rows = target.shape[0]
@@ -259,7 +260,8 @@
             target[rs, :] = one[rs, :] + two[rs, :]
             return carry
 
-        lax.fori_loop(0, rows // step, body, 0)
+        count = rows // step
+        lax.fori_loop(0, count, body, 0, unroll=math.gcd(count, 3) if count % 2 else 2)
 
     def flip(value, bit):
         weight = 1 << bit
@@ -800,7 +802,7 @@
                     r.yall[rows, :] = slots[m % 2][there, :].astype(BF)
                     return carry
 
-                lax.fori_loop(0, ROWS // 32, lower, 0)
+                lax.fori_loop(0, ROWS // 32, lower, 0, unroll=3)
                 if m + 2 < group:
                     fetch(m + 2).start()
 
@@ -1110,7 +1112,6 @@
         deep_make(CON)
 
     narrow_cotangent(r.a2, 1, ig[1], ib[1], 6, True, work_b)
-    wide_step(NAR, 1)
     gather_start(3)
     deep_core(CON)
     early, late = range(deep_parts // 2), range(deep_parts // 2, deep_parts)
@@ -1138,6 +1139,7 @@
         return carry
 
     lax.fori_loop(0, TAPS, unsample, 0, unroll=3)
+    wide_step(NAR, 1)
     z2(CON, [0])
     for s in range(SLOTS):
         put = r.tiny.at[1, chip, s]

time: 260 us -> 259 us (level)
  no operation moved by 1% of the time
where the time goes in v8:
time: 259 us; the launch traced here: 258 us
  Pallas kernels  257 us (99%)
    pallas_call x1, Pallas kernels, per_device(): pl.pallas_call(functools.partial(kernel, dp, outer, names), out_shape=[sp...  250 us
    pallas_call x1, Pallas kernels, per_device(): pl.pallas_call(functools.partial(deliver, dp, names), out_shape=[*finals....  7.33 us

profile of v8, /device:TPU:0, one launch (start us, length us, event | category | flops | bytes accessed | tf_op | source)
XLA Modules:
  0.0 258.1 jit_solution(16384524518652811031)
XLA Ops:
  0.7 250.0 %chain.1 = (bf16[288,2048]{1,0:T(8,128)(2,1)}, bf16[288,2048]{1,0:T(8,128)(2,1)}, f32[256,512]{1,0:T(8,128)}, f32[24,1536]{1,0:T(8,128)}, f32[576,512]{1,0:T(8,1...) custom-call(s32[32]{0:T(128)} %refs_0_.1, ...), custom_call_target="tpu_custom_call" | custom-call | tf_op jit(solution)/shard_map/chain/pallas_call | solution.py:1339
  250.6 7.3 %deliver.1 = (bf16[288,2048]{1,0:T(8,128)(2,1)}, bf16[288,2048]{1,0:T(8,128)(2,1)}, f32[256,512]{1,0:T(8,128)}, f32[576,512]{1,0:T(8,128)}, f32[256,512]{1,0:T(8...) custom-call(bf16[288,2048]{1,0:T(8,128)(2,1)} %get-tuple-element.39., ...), custom_call_target="tpu_custom_call" | custom-call | tf_op jit(solution)/shard_map/deliver/pallas_call | solution.py:1373

commit v9 on v8

--- a/solution.py
+++ b/solution.py
@@ -1106,10 +1106,10 @@
 
     def work_b():
         wide_send(NAR, 0)
-        z3(WID)
         wide_begin(EXP, r.dwide, r.hidden)
         gather_end(2)
         deep_make(CON)
+        z3(WID)
 
     narrow_cotangent(r.a2, 1, ig[1], ib[1], 6, True, work_b)
     gather_start(3)

time: 259 us -> 259 us (level)
  no operation moved by 1% of the time
where the time goes in v9:
time: 259 us
  Pallas kernels  258 us (100%)
    pallas_call x1, Pallas kernels, per_device(): pl.pallas_call(functools.partial(kernel, dp, outer, names), out_shape=[sp...  251 us
    pallas_call x1, Pallas kernels, per_device(): pl.pallas_call(functools.partial(deliver, dp, names), out_shape=[*finals....  7.33 us

profile of v9, /device:TPU:0, one launch (start us, length us, event | category | flops | bytes accessed | tf_op | source)
XLA Modules:
  0.0 258.8 jit_solution(4743980095698622556)
XLA Ops:
  0.7 250.7 %chain.1 = (bf16[288,2048]{1,0:T(8,128)(2,1)}, bf16[288,2048]{1,0:T(8,128)(2,1)}, f32[256,512]{1,0:T(8,128)}, f32[24,1536]{1,0:T(8,128)}, f32[576,512]{1,0:T(8,1...) custom-call(s32[32]{0:T(128)} %refs_0_.1, ...), custom_call_target="tpu_custom_call" | custom-call | tf_op jit(solution)/shard_map/chain/pallas_call | solution.py:1339
  251.3 7.3 %deliver.1 = (bf16[288,2048]{1,0:T(8,128)(2,1)}, bf16[288,2048]{1,0:T(8,128)(2,1)}, f32[256,512]{1,0:T(8,128)}, f32[576,512]{1,0:T(8,128)}, f32[256,512]{1,0:T(8...) custom-call(bf16[288,2048]{1,0:T(8,128)(2,1)} %get-tuple-element.39., ...), custom_call_target="tpu_custom_call" | custom-call | tf_op jit(solution)/shard_map/deliver/pallas_call | solution.py:1373
